TPU v7x, 128 devices: a whole 4x4x4 slice. The times are simulated.
128 devices in a mesh: px: 8 (over z, core), py: 16 (over x, y).
Axes of the slice: x: 4, y: 4, z: 4, core: 2. Of those that a mesh axis runs over, the one named last changes fastest.
Arguments:
- sources: bfloat16 [32, 64, 16, 256], P('px', 'py'), may hold values from -6 to 6
- near_codes: int32 [32, 64, 5], P('px', 'py'), may hold values from 0 to 8, as said below
- near_blocks: bfloat16 [32, 64, 5, 256, 256], P('px', 'py'), may hold values from -0.15625 to 0.15625
- basis: float32 [32, 64, 64, 256], P('px', 'py'), may hold values from -0.375 to 0.375
- transfer_one: float32 [32, 64, 64, 64], P('px', 'py'), may hold values from -0.375 to 0.375
- transfer_two: float32 [16, 32, 64, 64], P('px', 'py'), may hold values from -0.375 to 0.375
- transfer_three: float32 [8, 16, 64, 64], P('px', 'py'), may hold values from -0.375 to 0.375
- coupling_zero: float32 [32, 64, 8, 64, 64], P('px', 'py'), may hold values from -0.25 to 0.25
- codes_zero: int32 [32, 64, 8], P('px', 'py'), may hold values from 0 to 24, as said below
- coupling_one: float32 [16, 32, 8, 64, 64], P('px', 'py'), may hold values from -0.5 to 0.5
- codes_one: int32 [16, 32, 8], P('px', 'py'), may hold values from 0 to 24, as said below
- coupling_two: float32 [8, 16, 8, 64, 64], P('px', 'py'), may hold values from -1 to 1
- codes_two: int32 [8, 16, 8], P('px', 'py'), may hold values from 0 to 24, as said below
- coupling_three: float32 [4, 8, 8, 64, 64], replicated, may hold values from -2 to 2
- codes_three: int32 [4, 8, 8], replicated, may hold values from 0 to 24, as said below
Outputs:
- potential: float32 [32, 64, 16, 256], P('px', 'py')
Inputs may be any that keep to these rules, and one draw needn't show every extreme that they name: `near_codes`: entry 0 of every list is 4, the block itself; the other entries of a list are distinct codes of other blocks of its 3 x 3 neighbourhood. `codes_zero`: the entries of a list are distinct codes c with max(|c // 5 - 2|, |c % 5 - 2|) = 2. `codes_one`: the entries of a list are distinct codes c with max(|c // 5 - 2|, |c % 5 - 2|) = 2. `codes_two`: the entries of a list are distinct codes c with max(|c // 5 - 2|, |c % 5 - 2|) = 2. `codes_three`: the entries of a list are distinct codes c with max(|c // 5 - 2|, |c % 5 - 2|) = 2.
All inputs are finite; a program needn't handle non-finite values.
Results may differ from a plain program's by a relative error of at most 0.0003.
Values may be sent and summed in bfloat16 or wider, within the bound.
A program may use at most 128 MiB of HBM per device.

v0:
```python
import jax
import jax.numpy as jnp
from jax import lax
from jax.sharding import PartitionSpec as P

HIGHEST_PRECISION = lax.Precision.HIGHEST
CYCLE_CODES = (0, 1, 2, 3, 4, 5, 9, 10, 14, 15, 19, 20, 21, 22, 23, 24)
NEAR_CODES = (0, 1, 2, 3, 4, 5, 6, 7, 8)


def padded_2(cells, sides, width):
    for axis, dim in sides:
        count = lax.axis_size(axis)
        ends = count - 1
        head = lax.slice_in_dim(cells, 0, width, axis=dim)
        tail = lax.slice_in_dim(cells, cells.shape[dim] - width, cells.shape[dim], axis=dim)
        cells = jnp.concatenate(
            [
                lax.ppermute(tail, axis, [(i, (i + 1) % count) for i in range(ends)]),
                cells,
                lax.ppermute(head, axis, [((i + 1) % count, i) for i in range(ends)]),
            ],
            axis=dim,
        )
    return cells


def shifted(block, axis, distance):
    devices = range(lax.axis_size(axis))
    route = [(i - distance, i) for i in devices if i - distance in devices]
    return lax.ppermute(block, axis, route)


def swapped(value, axis, stride):
    mask = 2**stride
    pairs = [(source, source ^ mask) for source in range(lax.axis_size(axis))]
    return lax.ppermute(value, axis, pairs)


def select_codes(padded, codes, side, candidates):
    rows = codes.shape[0]
    columns = codes.shape[1]
    trailing = padded.shape[2:]
    result = jnp.zeros(codes.shape + trailing, padded.dtype)
    for code in candidates:
        start_row = code // side
        start_column = code % side
        piece = padded[start_row : start_row + rows, start_column : start_column + columns]
        marks = (codes == code).reshape(codes.shape + (1,) * len(trailing))
        result = result + jnp.where(marks, piece[:, :, None], jnp.zeros((), padded.dtype))
    return result


def lift(panel, transfer):
    moved = jnp.einsum("ijrn,ijnm->ijrm", panel, transfer, precision=HIGHEST_PRECISION)
    rows = panel.shape[0] // 2
    columns = panel.shape[1] // 2
    return moved.reshape(rows, 2, columns, 2, moved.shape[2], moved.shape[3]).sum(axis=(1, 3))


def rim_halo(flat):
    return padded_2(flat, (("px", 0), ("py", 1)), 2)


def couple_padded(padded, coupling, codes, rhs_count, rank_count):
    chosen = select_codes(padded, codes, 5, CYCLE_CODES)
    chosen = chosen.reshape(codes.shape[0], codes.shape[1], codes.shape[2], rhs_count, rank_count)
    return jnp.einsum("ijkmn,ijkrn->ijrm", coupling, chosen, precision=HIGHEST_PRECISION)


def couple_window(window, coupling, codes, rhs_count, rank_count):
    table = window.reshape(25, window.shape[2])
    indicator = (codes[:, None] == jnp.arange(25, dtype=jnp.int32)[None, :]).astype(jnp.float32)
    chosen = jnp.dot(indicator, table, precision=HIGHEST_PRECISION)
    chosen = chosen.reshape(codes.shape[0], rhs_count, rank_count)
    return jnp.einsum("kmn,krn->rm", coupling, chosen, precision=HIGHEST_PRECISION)


def window_shifts(flat, stride):
    lines = []
    for offset in (-2, -1, 0, 1, 2):
        if offset == 0:
            lines.append(flat)
        else:
            lines.append(shifted(flat, "px", -offset * stride))
    stacked = jnp.stack(lines)
    grid_lines = []
    for offset in (-2, -1, 0, 1, 2):
        if offset == 0:
            grid_lines.append(stacked)
        else:
            grid_lines.append(shifted(stacked, "py", -offset * stride))
    return jnp.stack(grid_lines, axis=1)


def on_device(
    sources,
    near_codes,
    near_blocks,
    basis,
    transfer_one,
    transfer_two,
    transfer_three,
    coupling_zero,
    codes_zero,
    coupling_one,
    codes_one,
    coupling_two,
    codes_two,
    coupling_three,
    codes_three,
):
    padded = padded_2(sources, (("px", 0), ("py", 1)), 1)
    neighbours = select_codes(padded, near_codes, 3, NEAR_CODES)
    near_field = jnp.einsum(
        "ijkab,ijkrb->ijra", near_blocks, neighbours, preferred_element_type=jnp.float32
    )
    panel_zero = jnp.einsum(
        "ijrb,ijmb->ijrm", sources.astype(jnp.float32), basis, precision=HIGHEST_PRECISION
    )
    panel_one = lift(panel_zero, transfer_one)
    panel_two = lift(panel_one, transfer_two)
    share_three = jnp.einsum(
        "rn,nm->rm", panel_two[0, 0], transfer_three[0, 0], precision=HIGHEST_PRECISION
    )
    rhs_count, rank_count = share_three.shape
    width = rhs_count * rank_count
    rows_zero, columns_zero = (panel_zero.shape[0], panel_zero.shape[1])
    rows_one, columns_one = (panel_one.shape[0], panel_one.shape[1])
    flat_zero = panel_zero.reshape(rows_zero, columns_zero, width)
    flat_one = panel_one.reshape(rows_one, columns_one, width)
    padded_zero = rim_halo(flat_zero)
    padded_one = rim_halo(flat_one)
    coupled_zero = couple_padded(padded_zero, coupling_zero, codes_zero, rhs_count, rank_count)
    coupled_one = couple_padded(padded_one, coupling_one, codes_one, rhs_count, rank_count)
    row_index = lax.axis_index("px") // 2
    column_index = lax.axis_index("py") // 2
    own_coupling = lax.dynamic_slice(
        coupling_three, (row_index, column_index, 0, 0, 0), (1, 1) + coupling_three.shape[2:]
    )[0, 0]
    own_codes = lax.dynamic_slice(
        codes_three, (row_index, column_index, 0), (1, 1, codes_three.shape[2])
    )[0, 0]
    flat_two = panel_two.reshape(width)
    flat_share = share_three.reshape(width)
    window_two = window_shifts(flat_two, 1)
    paired = flat_share + swapped(flat_share, "px", 0)
    panel_three = paired + swapped(paired, "py", 0)
    window_three = window_shifts(panel_three, 2)
    coupled_two = couple_window(
        window_two, coupling_two[0, 0], codes_two[0, 0], rhs_count, rank_count
    )
    field_three = couple_window(window_three, own_coupling, own_codes, rhs_count, rank_count)
    field_two = coupled_two + jnp.einsum(
        "nm,rm->rn", transfer_three[0, 0], field_three, precision=HIGHEST_PRECISION
    )
    field_one = coupled_one + jnp.einsum(
        "ijnm,rm->ijrn", transfer_two, field_two, precision=HIGHEST_PRECISION
    )
    spread = jnp.repeat(jnp.repeat(field_one, 2, axis=0), 2, axis=1)
    field_zero = coupled_zero + jnp.einsum(
        "ijnm,ijrm->ijrn", transfer_one, spread, precision=HIGHEST_PRECISION
    )
    far_field = jnp.einsum("ijmb,ijrm->ijrb", basis, field_zero, precision=HIGHEST_PRECISION)
    return near_field + far_field


def solution(mesh):
    placed = (
        P("px", "py", None, None),
        P("px", "py", None),
        P("px", "py", None, None, None),
        P("px", "py", None, None),
        P("px", "py", None, None),
        P("px", "py", None, None),
        P("px", "py", None, None),
        P("px", "py", None, None, None),
        P("px", "py", None),
        P("px", "py", None, None, None),
        P("px", "py", None),
        P("px", "py", None, None, None),
        P("px", "py", None),
        P(),
        P(),
    )
    return jax.shard_map(
        on_device, mesh=mesh, in_specs=placed, out_specs=P("px", "py", None, None), check_vma=False
    )
```

profile of v0, /device:TPU:100, one launch (start us, length us, event | category | flops | bytes accessed | tf_op | source)
XLA Modules:
  0.0 145.4 jit_solution(15908645720152795952)
XLA Ops:
  1.2 1.5 %fusion.209 = f32[4,4,16,64]{3,2,1,0:T(8,128)S(1)} fusion(bf16[4,4,16,256]{3,2,1,0:T(8,128)(2,1)} %param.15, f32[4,4,64,256]{3,2,1,0:T(8,128)S(1)} %copy-done), kind=kOutput, calls=%fused_computation.313 | convolution fusion | flops 50331648 | bytes 1245184 | tf_op jit(solution)/shard_map/ijrb,ijmb->ijrm/dot_general | solution.py:118
  2.7 1.6 %fusion.210 = f32[4,4,16,64]{3,2,1,0:T(8,128)S(1)} fusion(f32[4,4,16,64]{3,2,1,0:T(8,128)S(1)} %fusion.209, f32[4,4,64,64]{3,2,1,0:T(8,128)} %param.19), kind=kOutput, calls=%fused_computation.314 | convolution fusion | flops 12582912 | bytes 393216 | tf_op jit(solution)/shard_map/ijrn,ijnm->ijrm/dot_general | solution.py:55
  6.9 1.9 %collective-permute-start.13 = (f32[1024]{0:T(1024)S(1)}, f32[1024]{0:T(1024)S(1)}, u32[]{:S(2)}, u32[]{:S(2)}) collective-permute-start(f32[1024]{0:T(1024)S(1)} %reshape.232), channel_id=1, source_target_pairs={{0,16},{16,32},{32,48},{48,64},{64,80},{80,96},{96,112},{1,17},{17... | collective-permute-start | bytes 12296 | tf_op jit(solution)/shard_map/ppermute | solution.py:31
  8.8 3.7 %collective-permute-start.14 = (f32[1024]{0:T(1024)S(1)}, f32[1024]{0:T(1024)S(1)}, u32[]{:S(2)}, u32[]{:S(2)}) collective-permute-start(f32[1024]{0:T(1024)S(1)} %reshape.232), channel_id=1, source_target_pairs={{16,0},{32,16},{48,32},{64,48},{80,64},{96,80},{112,96},{17,1},{33... | collective-permute-start | bytes 12296 | tf_op jit(solution)/shard_map/ppermute | solution.py:31
  12.5 4.5 %collective-permute-start.15 = (f32[1024]{0:T(1024)S(1)}, f32[1024]{0:T(1024)S(1)}, u32[]{:S(2)}, u32[]{:S(2)}) collective-permute-start(f32[1024]{0:T(1024)S(1)} %reshape.232), channel_id=1, source_target_pairs={{32,0},{48,16},{64,32},{80,48},{96,64},{112,80},{33,1},{49,17},{65... | collective-permute-start | bytes 12296 | tf_op jit(solution)/shard_map/ppermute | solution.py:31
  21.5 1.7 %collective-permute-start.21 = (f32[1024]{0:T(1024)S(1)}, f32[1024]{0:T(1024)S(1)}, u32[]{:S(2)}, u32[]{:S(2)}) collective-permute-start(f32[1024]{0:T(1024)S(1)} %add.212), channel_id=1, source_target_pairs={{0,1},{1,0},{2,3},{3,2},{4,5},{5,4},{6,7},{7,6},{8,9},{9,8},{10,11... | collective-permute-start | bytes 12296 | tf_op jit(solution)/shard_map/ppermute | solution.py:37
  25.2 1.9 %collective-permute-start.8 = (f32[2,2,1024]{2,1,0:T(2,128)S(1)}, f32[2,2,1024]{2,1,0:T(2,128)S(1)}, u32[]{:S(2)}, u32[]{:S(2)}) collective-permute-start(f32[2,2,1024]{2,1,0:T(2,128)S(1)} %reshape.231), channel_id=1, source_target_pairs={{0,16},{16,32},{32,48},{48,64},{64,80},{80,96},{96,112},{1,17},{17... | collective-permute-start | bytes 49160 | tf_op jit(solution)/shard_map/ppermute | solution.py:19
  29.7 4.5 %collective-permute-start.24 = (f32[1024]{0:T(1024)S(1)}, f32[1024]{0:T(1024)S(1)}, u32[]{:S(2)}, u32[]{:S(2)}) collective-permute-start(f32[1024]{0:T(1024)S(1)} %add.213), channel_id=1, source_target_pairs={{32,0},{48,16},{64,32},{80,48},{96,64},{112,80},{33,1},{49,17},{65... | collective-permute-start | bytes 12296 | tf_op jit(solution)/shard_map/ppermute | solution.py:31
  34.3 6.0 %collective-permute-start.25 = (f32[1024]{0:T(1024)S(1)}, f32[1024]{0:T(1024)S(1)}, u32[]{:S(2)}, u32[]{:S(2)}) collective-permute-start(f32[1024]{0:T(1024)S(1)} %add.213), channel_id=1, source_target_pairs={{64,0},{80,16},{96,32},{112,48},{65,1},{81,17},{97,33},{113,49},{6... | collective-permute-start | bytes 12296 | tf_op jit(solution)/shard_map/ppermute | solution.py:31
  41.5 1.9 %collective-permute-start.9 = (f32[2,2,1024]{2,1,0:T(2,128)S(1)}, f32[2,2,1024]{2,1,0:T(2,128)S(1)}, u32[]{:S(2)}, u32[]{:S(2)}) collective-permute-start(f32[2,2,1024]{2,1,0:T(2,128)S(1)} %reshape.231), channel_id=1, source_target_pairs={{16,0},{32,16},{48,32},{64,48},{80,64},{96,80},{112,96},{17,1},{33... | collective-permute-start | bytes 49160 | tf_op jit(solution)/shard_map/ppermute | solution.py:21
  43.4 2.4 %collective-permute-start.4 = (f32[2,4,1024]{2,1,0:T(4,128)S(1)}, f32[2,4,1024]{2,1,0:T(4,128)S(1)}, u32[]{:S(2)}, u32[]{:S(2)}) collective-permute-start(f32[2,4,1024]{2,1,0:T(4,128)S(1)} %slice.185), channel_id=1, source_target_pairs={{0,16},{16,32},{32,48},{48,64},{64,80},{80,96},{96,112},{1,17},{17... | collective-permute-start | bytes 98312 | tf_op jit(solution)/shard_map/ppermute | solution.py:19
  45.9 5.1 %collective-permute-start.16 = (f32[5,1024]{1,0:T(8,128)S(1)}, f32[5,1024]{1,0:T(8,128)S(1)}, u32[]{:S(2)}, u32[]{:S(2)}) collective-permute-start(f32[5,1024]{1,0:T(8,128)S(1)} %stack.73), channel_id=1, source_target_pairs={{0,2},{1,3},{2,4},{3,5},{4,6},{5,7},{6,8},{7,9},{8,10},{9,11},{10,... | collective-permute-start | bytes 61448 | tf_op jit(solution)/shard_map/ppermute | solution.py:31
  51.0 2.6 %collective-permute-start.17 = (f32[5,1024]{1,0:T(8,128)S(1)}, f32[5,1024]{1,0:T(8,128)S(1)}, u32[]{:S(2)}, u32[]{:S(2)}) collective-permute-start(f32[5,1024]{1,0:T(8,128)S(1)} %stack.73), channel_id=1, source_target_pairs={{0,1},{1,2},{2,3},{3,4},{4,5},{5,6},{6,7},{7,8},{8,9},{9,10},{10,1... | collective-permute-start | bytes 61448 | tf_op jit(solution)/shard_map/ppermute | solution.py:31
  53.7 5.4 %collective-permute-start.18 = (f32[5,1024]{1,0:T(8,128)S(1)}, f32[5,1024]{1,0:T(8,128)S(1)}, u32[]{:S(2)}, u32[]{:S(2)}) collective-permute-start(f32[5,1024]{1,0:T(8,128)S(1)} %stack.73), channel_id=1, source_target_pairs={{1,0},{2,1},{3,2},{4,3},{5,4},{6,5},{7,6},{8,7},{9,8},{10,9},{11,1... | collective-permute-start | bytes 61448 | tf_op jit(solution)/shard_map/ppermute | solution.py:31
  59.1 1.9 %collective-permute-start.19 = (f32[5,1024]{1,0:T(8,128)S(1)}, f32[5,1024]{1,0:T(8,128)S(1)}, u32[]{:S(2)}, u32[]{:S(2)}) collective-permute-start(f32[5,1024]{1,0:T(8,128)S(1)} %stack.73), channel_id=1, source_target_pairs={{2,0},{3,1},{4,2},{5,3},{6,4},{7,5},{8,6},{9,7},{10,8},{11,9},{12,... | collective-permute-start | bytes 61448 | tf_op jit(solution)/shard_map/ppermute | solution.py:31
  61.2 2.3 %collective-permute-start.5 = (f32[2,4,1024]{2,1,0:T(4,128)S(1)}, f32[2,4,1024]{2,1,0:T(4,128)S(1)}, u32[]{:S(2)}, u32[]{:S(2)}) collective-permute-start(f32[2,4,1024]{2,1,0:T(4,128)S(1)} %slice.187), channel_id=1, source_target_pairs={{16,0},{32,16},{48,32},{64,48},{80,64},{96,80},{112,96},{17,1},{33... | collective-permute-start | bytes 98312 | tf_op jit(solution)/shard_map/ppermute | solution.py:21
  63.6 2.0 %collective-permute-start = (bf16[1,4,16,256]{3,2,1,0:T(8,128)(2,1)S(1)}, bf16[1,4,16,256]{3,2,1,0:T(8,128)(2,1)S(1)}, u32[]{:S(2)}, u32[]{:S(2)}) collective-permute-start(bf16[1,4,16,256]{3,2,1,0:T(8,128)(2,1)S(1)} %get-tuple-element.34), channel_id=1, source_target_pairs={{0,16},{16,32},{32,48},{48,64},{64,80},{80,96},{96,112},{1,17},{17... | collective-permute-start | bytes 98312 | tf_op jit(solution)/shard_map/ppermute | solution.py:19
  65.6 3.6 %collective-permute-start.1 = (bf16[1,4,16,256]{3,2,1,0:T(8,128)(2,1)S(1)}, bf16[1,4,16,256]{3,2,1,0:T(8,128)(2,1)S(1)}, u32[]{:S(2)}, u32[]{:S(2)}) collective-permute-start(bf16[1,4,16,256]{3,2,1,0:T(8,128)(2,1)S(1)} %get-tuple-element.33), channel_id=1, source_target_pairs={{16,0},{32,16},{48,32},{64,48},{80,64},{96,80},{112,96},{17,1},{33... | collective-permute-start | bytes 98312 | tf_op jit(solution)/shard_map/ppermute | solution.py:21
  69.2 3.1 %collective-permute-start.26 = (f32[5,1024]{1,0:T(8,128)S(1)}, f32[5,1024]{1,0:T(8,128)S(1)}, u32[]{:S(2)}, u32[]{:S(2)}) collective-permute-start(f32[5,1024]{1,0:T(8,128)S(1)} %stack.85), channel_id=1, source_target_pairs={{0,4},{1,5},{2,6},{3,7},{4,8},{5,9},{6,10},{7,11},{8,12},{9,13},{1... | collective-permute-start | bytes 61448 | tf_op jit(solution)/shard_map/ppermute | solution.py:31
  74.8 5.1 %collective-permute-start.27 = (f32[5,1024]{1,0:T(8,128)S(1)}, f32[5,1024]{1,0:T(8,128)S(1)}, u32[]{:S(2)}, u32[]{:S(2)}) collective-permute-start(f32[5,1024]{1,0:T(8,128)S(1)} %stack.85), channel_id=1, source_target_pairs={{0,2},{1,3},{2,4},{3,5},{4,6},{5,7},{6,8},{7,9},{8,10},{9,11},{10,... | collective-permute-start | bytes 61448 | tf_op jit(solution)/shard_map/ppermute | solution.py:31
  80.0 3.1 %collective-permute-start.28 = (f32[5,1024]{1,0:T(8,128)S(1)}, f32[5,1024]{1,0:T(8,128)S(1)}, u32[]{:S(2)}, u32[]{:S(2)}) collective-permute-start(f32[5,1024]{1,0:T(8,128)S(1)} %stack.85), channel_id=1, source_target_pairs={{2,0},{3,1},{4,2},{5,3},{6,4},{7,5},{8,6},{9,7},{10,8},{11,9},{12,... | collective-permute-start | bytes 61448 | tf_op jit(solution)/shard_map/ppermute | solution.py:31
  83.3 2.7 %collective-permute-start.29 = (f32[5,1024]{1,0:T(8,128)S(1)}, f32[5,1024]{1,0:T(8,128)S(1)}, u32[]{:S(2)}, u32[]{:S(2)}) collective-permute-start(f32[5,1024]{1,0:T(8,128)S(1)} %stack.85), channel_id=1, source_target_pairs={{4,0},{5,1},{6,2},{7,3},{8,4},{9,5},{10,6},{11,7},{12,8},{13,9},{1... | collective-permute-start | bytes 61448 | tf_op jit(solution)/shard_map/ppermute | solution.py:31
  86.0 2.8 %collective-permute-start.10 = (f32[6,2,1024]{2,1,0:T(2,128)S(1)}, f32[6,2,1024]{2,1,0:T(2,128)S(1)}, u32[]{:S(2)}, u32[]{:S(2)}) collective-permute-start(f32[6,2,1024]{2,1,0:T(2,128)S(1)} %constant_dynamic-update-slice_fusion.6), channel_id=1, source_target_pairs={{0,1},{1,2},{2,3},{3,4},{4,5},{5,6},{6,7},{7,8},{8,9},{9,10},{10,1... | collective-permute-start | bytes 147464 | tf_op jit(solution)/shard_map/ppermute | solution.py:19
  88.8 5.2 %collective-permute-start.11 = (f32[6,2,1024]{2,1,0:T(2,128)S(1)}, f32[6,2,1024]{2,1,0:T(2,128)S(1)}, u32[]{:S(2)}, u32[]{:S(2)}) collective-permute-start(f32[6,2,1024]{2,1,0:T(2,128)S(1)} %constant_dynamic-update-slice_fusion.6), channel_id=1, source_target_pairs={{1,0},{2,1},{3,2},{4,3},{5,4},{6,5},{7,6},{8,7},{9,8},{10,9},{11,1... | collective-permute-start | bytes 147464 | tf_op jit(solution)/shard_map/ppermute | solution.py:21
  94.1 1.9 %collective-permute-start.6 = (f32[8,2,1024]{2,1,0:T(2,128)S(1)}, f32[8,2,1024]{2,1,0:T(2,128)S(1)}, u32[]{:S(2)}, u32[]{:S(2)}) collective-permute-start(f32[8,2,1024]{2,1,0:T(2,128)S(1)} %get-tuple-element.35), channel_id=1, source_target_pairs={{0,1},{1,2},{2,3},{3,4},{4,5},{5,6},{6,7},{7,8},{8,9},{9,10},{10,1... | collective-permute-start | bytes 196616 | tf_op jit(solution)/shard_map/ppermute | solution.py:19
  96.0 6.0 %collective-permute-start.7 = (f32[8,2,1024]{2,1,0:T(2,128)S(1)}, f32[8,2,1024]{2,1,0:T(2,128)}, u32[]{:S(2)}, u32[]{:S(2)}) collective-permute-start(f32[8,2,1024]{2,1,0:T(2,128)S(1)} %get-tuple-element.36), channel_id=1, source_target_pairs={{1,0},{2,1},{3,2},{4,3},{5,4},{6,5},{7,6},{8,7},{9,8},{10,9},{11,1... | collective-permute-start | bytes 196616 | tf_op jit(solution)/shard_map/ppermute | solution.py:21
  102.6 1.8 %pad_maximum_fusion.3 = (bf16[4,4,16,256]{3,2,1,0:T(8,128)(2,1)}, bf16[4,4,16,256]{3,2,1,0:T(8,128)(2,1)}, bf16[6,4,16,256]{3,2,1,0:T(8,128)(2,1)S(1)}) fusion(bf16[4,4,16,256]{3,2,1,0:T(8,128)(2,1)} %param.15, bf16[1,4,16,256]{3,2,1,0:T(8,128)(2,1)S(1)} %collective-permute-done, bf16[1,4,16,256]{3,2,1,0:T(8,128)(2,1)S(1)} %collective-permute-done.1, ...), kind=kLoop, calls=%fused_computation.189 | loop fusion | flops 524288 | bytes 589824 | tf_op jit(solution)/shard_map/concatenate | solution.py:17
  104.4 1.9 %collective-permute-start.2 = (bf16[6,1,16,256]{3,2,1,0:T(8,128)(2,1)S(1)}, bf16[6,1,16,256]{3,2,1,0:T(8,128)(2,1)S(1)}, u32[]{:S(2)}, u32[]{:S(2)}) collective-permute-start(bf16[6,1,16,256]{3,2,1,0:T(8,128)(2,1)S(1)} %get-tuple-element.14), channel_id=1, source_target_pairs={{0,1},{1,2},{2,3},{3,4},{4,5},{5,6},{6,7},{7,8},{8,9},{9,10},{10,1... | collective-permute-start | bytes 147464 | tf_op jit(solution)/shard_map/ppermute | solution.py:19
  108.1 6.2 %collective-permute-start.3 = (bf16[6,1,16,256]{3,2,1,0:T(8,128)(2,1)S(1)}, bf16[6,1,16,256]{3,2,1,0:T(8,128)(2,1)S(1)}, u32[]{:S(2)}, u32[]{:S(2)}) collective-permute-start(bf16[6,1,16,256]{3,2,1,0:T(8,128)(2,1)S(1)} %get-tuple-element.15), channel_id=1, source_target_pairs={{1,0},{2,1},{3,2},{4,3},{5,4},{6,5},{7,6},{8,7},{9,8},{10,9},{11,1... | collective-permute-start | bytes 147464 | tf_op jit(solution)/shard_map/ppermute | solution.py:21
  115.6 2.7 %convolution_bitcast_fusion.3 = f32[2,2,16,64]{3,2,1,0:T(8,128)S(1)} fusion(f32[2,2,8,64,64]{4,3,2,1,0:T(8,128)} %param.24, f32[2,2,16,64]{3,2,1,0:T(8,128)S(1)} %broadcast_in_dim.706, f32[2,2,16,64]{3,2,1,0:T(8,128)S(1)} %broadcast_in_dim.703, f32[2,2,16,64]{3,2,1,0:T(8,128)S(1)} %broadcast_in_dim.700, f32[2,2,16,64]{3,2,1,0:T(8,128)S(1)} %broadcast_in_dim.697, ...), kind=kOutput, calls=%fused_computation.6 | convolution fusion | flops 26181632 | bytes 803328 | tf_op jit(solution)/shard_map/ijkmn,ijkrn->ijrm/dot_general | solution.py:68
  128.3 9.1 %convolution_bitcast_fusion.1 = f32[4,4,16,64]{3,2,1,0:T(8,128)S(1)} fusion(f32[4,4,8,64,64]{4,3,2,1,0:T(8,128)} %param.22, f32[4,4,16,64]{3,2,1,0:T(8,128)S(1)} %broadcast_in_dim.657, f32[4,4,16,64]{3,2,1,0:T(8,128)} %broadcast_in_dim.654, f32[4,4,16,64]{3,2,1,0:T(8,128)S(1)} %broadcast_in_dim.651, f32[4,4,16,64]{3,2,1,0:T(8,128)} %broadcast_in_dim.648, ...), kind=kOutput, calls=%fused_computation.3 | convolution fusion | flops 104726528 | bytes 3213312 | tf_op jit(solution)/shard_map/ijkmn,ijkrn->ijrm/dot_general | solution.py:68
  139.0 6.4 %fusion = f32[4,4,16,256]{3,2,1,0:T(8,128)} fusion(f32[4,4,16,256]{3,2,1,0:T(8,128)S(1)} %fusion.211, bf16[4,4,5,256,256]{4,3,2,1,0:T(8,128)(2,1)} %param.17, pred[4,4,5]{2,1,0:T(4,128)(4,1)} %get-tuple-element.65, pred[4,4,5]{2,1,0:T(4,128)(4,1)} %get-tuple-element.66, pred[4,4,5]{2,1,0:T(4,128)(4,1)} %get-tuple-element.59, ...), kind=kOutput, calls=%fused_computation.1 | convolution fusion | flops 173408256 | bytes 12190416 | tf_op jit(solution)/shard_map/ijkab,ijkrb->ijra/dot_general | solution.py:115
  (136 shorter events, 31.9 us)
Async XLA Ops:
  0.0 118.3 %copy-start.3 = (f32[2,2,64,64]{3,2,1,0:T(8,128)S(1)}, f32[2,2,64,64]{3,2,1,0:T(8,128)}, u32[]{:S(2)}) copy-start(f32[2,2,64,64]{3,2,1,0:T(8,128)} %param.20) | copy-start | bytes 196612
  0.0 107.8 %copy-start.4 = (f32[1,1,64,64]{3,2,1,0:T(8,128)S(1)}, f32[1,1,64,64]{3,2,1,0:T(8,128)}, u32[]{:S(2)}) copy-start(f32[1,1,64,64]{3,2,1,0:T(8,128)} %param.21) | copy-start | bytes 49156
  5.6 21.5 %collective-permute-start.12 = (f32[1024]{0:T(1024)S(1)}, f32[1024]{0:T(1024)S(1)}, u32[]{:S(2)}, u32[]{:S(2)}) collective-permute-start(f32[1024]{0:T(1024)S(1)} %reshape.232), channel_id=1, source_target_pairs={{0,32},{16,48},{32,64},{48,80},{64,96},{80,112},{1,33},{17,49},{33... | collective-permute-start | bytes 12296 | tf_op jit(solution)/shard_map/ppermute | solution.py:31
  6.9 21.5 %collective-permute-start.13 = (f32[1024]{0:T(1024)S(1)}, f32[1024]{0:T(1024)S(1)}, u32[]{:S(2)}, u32[]{:S(2)}) collective-permute-start(f32[1024]{0:T(1024)S(1)} %reshape.232), channel_id=1, source_target_pairs={{0,16},{16,32},{32,48},{48,64},{64,80},{80,96},{96,112},{1,17},{17... | collective-permute-start | bytes 12296 | tf_op jit(solution)/shard_map/ppermute | solution.py:31
  8.8 20.9 %collective-permute-start.14 = (f32[1024]{0:T(1024)S(1)}, f32[1024]{0:T(1024)S(1)}, u32[]{:S(2)}, u32[]{:S(2)}) collective-permute-start(f32[1024]{0:T(1024)S(1)} %reshape.232), channel_id=1, source_target_pairs={{16,0},{32,16},{48,32},{64,48},{80,64},{96,80},{112,96},{17,1},{33... | collective-permute-start | bytes 12296 | tf_op jit(solution)/shard_map/ppermute | solution.py:31
  12.5 21.8 %collective-permute-start.15 = (f32[1024]{0:T(1024)S(1)}, f32[1024]{0:T(1024)S(1)}, u32[]{:S(2)}, u32[]{:S(2)}) collective-permute-start(f32[1024]{0:T(1024)S(1)} %reshape.232), channel_id=1, source_target_pairs={{32,0},{48,16},{64,32},{80,48},{96,64},{112,80},{33,1},{49,17},{65... | collective-permute-start | bytes 12296 | tf_op jit(solution)/shard_map/ppermute | solution.py:31
  18.0 3.5 %collective-permute-start.20 = (f32[1024]{0:T(1024)S(1)}, f32[1024]{0:T(1024)S(1)}, u32[]{:S(2)}, u32[]{:S(2)}) collective-permute-start(f32[1024]{0:T(1024)S(1)} %reshape.234), channel_id=1, source_target_pairs={{0,16},{16,0},{32,48},{48,32},{64,80},{80,64},{96,112},{112,96},{1... | collective-permute-start | bytes 12296 | tf_op jit(solution)/shard_map/ppermute | solution.py:37
  21.5 3.7 %collective-permute-start.21 = (f32[1024]{0:T(1024)S(1)}, f32[1024]{0:T(1024)S(1)}, u32[]{:S(2)}, u32[]{:S(2)}) collective-permute-start(f32[1024]{0:T(1024)S(1)} %add.212), channel_id=1, source_target_pairs={{0,1},{1,0},{2,3},{3,2},{4,5},{5,4},{6,7},{7,6},{8,9},{9,8},{10,11... | collective-permute-start | bytes 12296 | tf_op jit(solution)/shard_map/ppermute | solution.py:37
  25.2 28.5 %collective-permute-start.8 = (f32[2,2,1024]{2,1,0:T(2,128)S(1)}, f32[2,2,1024]{2,1,0:T(2,128)S(1)}, u32[]{:S(2)}, u32[]{:S(2)}) collective-permute-start(f32[2,2,1024]{2,1,0:T(2,128)S(1)} %reshape.231), channel_id=1, source_target_pairs={{0,16},{16,32},{32,48},{48,64},{64,80},{80,96},{96,112},{1,17},{17... | collective-permute-start | bytes 49160 | tf_op jit(solution)/shard_map/ppermute | solution.py:19
  27.1 14.4 %collective-permute-start.22 = (f32[1024]{0:T(1024)S(1)}, f32[1024]{0:T(1024)S(1)}, u32[]{:S(2)}, u32[]{:S(2)}) collective-permute-start(f32[1024]{0:T(1024)S(1)} %add.213), channel_id=1, source_target_pairs={{0,64},{16,80},{32,96},{48,112},{1,65},{17,81},{33,97},{49,113},{2... | collective-permute-start | bytes 12296 | tf_op jit(solution)/shard_map/ppermute | solution.py:31
  28.4 15.0 %collective-permute-start.23 = (f32[1024]{0:T(1024)S(1)}, f32[1024]{0:T(1024)S(1)}, u32[]{:S(2)}, u32[]{:S(2)}) collective-permute-start(f32[1024]{0:T(1024)S(1)} %add.213), channel_id=1, source_target_pairs={{0,32},{16,48},{32,64},{48,80},{64,96},{80,112},{1,33},{17,49},{33... | collective-permute-start | bytes 12296 | tf_op jit(solution)/shard_map/ppermute | solution.py:31
  29.7 16.1 %collective-permute-start.24 = (f32[1024]{0:T(1024)S(1)}, f32[1024]{0:T(1024)S(1)}, u32[]{:S(2)}, u32[]{:S(2)}) collective-permute-start(f32[1024]{0:T(1024)S(1)} %add.213), channel_id=1, source_target_pairs={{32,0},{48,16},{64,32},{80,48},{96,64},{112,80},{33,1},{49,17},{65... | collective-permute-start | bytes 12296 | tf_op jit(solution)/shard_map/ppermute | solution.py:31
  34.3 16.7 %collective-permute-start.25 = (f32[1024]{0:T(1024)S(1)}, f32[1024]{0:T(1024)S(1)}, u32[]{:S(2)}, u32[]{:S(2)}) collective-permute-start(f32[1024]{0:T(1024)S(1)} %add.213), channel_id=1, source_target_pairs={{64,0},{80,16},{96,32},{112,48},{65,1},{81,17},{97,33},{113,49},{6... | collective-permute-start | bytes 12296 | tf_op jit(solution)/shard_map/ppermute | solution.py:31
  41.5 17.6 %collective-permute-start.9 = (f32[2,2,1024]{2,1,0:T(2,128)S(1)}, f32[2,2,1024]{2,1,0:T(2,128)S(1)}, u32[]{:S(2)}, u32[]{:S(2)}) collective-permute-start(f32[2,2,1024]{2,1,0:T(2,128)S(1)} %reshape.231), channel_id=1, source_target_pairs={{16,0},{32,16},{48,32},{64,48},{80,64},{96,80},{112,96},{17,1},{33... | collective-permute-start | bytes 49160 | tf_op jit(solution)/shard_map/ppermute | solution.py:21
  43.4 31.4 %collective-permute-start.4 = (f32[2,4,1024]{2,1,0:T(4,128)S(1)}, f32[2,4,1024]{2,1,0:T(4,128)S(1)}, u32[]{:S(2)}, u32[]{:S(2)}) collective-permute-start(f32[2,4,1024]{2,1,0:T(4,128)S(1)} %slice.185), channel_id=1, source_target_pairs={{0,16},{16,32},{32,48},{48,64},{64,80},{80,96},{96,112},{1,17},{17... | collective-permute-start | bytes 98312 | tf_op jit(solution)/shard_map/ppermute | solution.py:19
  45.9 15.3 %collective-permute-start.16 = (f32[5,1024]{1,0:T(8,128)S(1)}, f32[5,1024]{1,0:T(8,128)S(1)}, u32[]{:S(2)}, u32[]{:S(2)}) collective-permute-start(f32[5,1024]{1,0:T(8,128)S(1)} %stack.73), channel_id=1, source_target_pairs={{0,2},{1,3},{2,4},{3,5},{4,6},{5,7},{6,8},{7,9},{8,10},{9,11},{10,... | collective-permute-start | bytes 61448 | tf_op jit(solution)/shard_map/ppermute | solution.py:31
  51.0 12.6 %collective-permute-start.17 = (f32[5,1024]{1,0:T(8,128)S(1)}, f32[5,1024]{1,0:T(8,128)S(1)}, u32[]{:S(2)}, u32[]{:S(2)}) collective-permute-start(f32[5,1024]{1,0:T(8,128)S(1)} %stack.73), channel_id=1, source_target_pairs={{0,1},{1,2},{2,3},{3,4},{4,5},{5,6},{6,7},{7,8},{8,9},{9,10},{10,1... | collective-permute-start | bytes 61448 | tf_op jit(solution)/shard_map/ppermute | solution.py:31
  53.7 11.9 %collective-permute-start.18 = (f32[5,1024]{1,0:T(8,128)S(1)}, f32[5,1024]{1,0:T(8,128)S(1)}, u32[]{:S(2)}, u32[]{:S(2)}) collective-permute-start(f32[5,1024]{1,0:T(8,128)S(1)} %stack.73), channel_id=1, source_target_pairs={{1,0},{2,1},{3,2},{4,3},{5,4},{6,5},{7,6},{8,7},{9,8},{10,9},{11,1... | collective-permute-start | bytes 61448 | tf_op jit(solution)/shard_map/ppermute | solution.py:31
  59.1 10.1 %collective-permute-start.19 = (f32[5,1024]{1,0:T(8,128)S(1)}, f32[5,1024]{1,0:T(8,128)S(1)}, u32[]{:S(2)}, u32[]{:S(2)}) collective-permute-start(f32[5,1024]{1,0:T(8,128)S(1)} %stack.73), channel_id=1, source_target_pairs={{2,0},{3,1},{4,2},{5,3},{6,4},{7,5},{8,6},{9,7},{10,8},{11,9},{12,... | collective-permute-start | bytes 61448 | tf_op jit(solution)/shard_map/ppermute | solution.py:31
  61.2 18.8 %collective-permute-start.5 = (f32[2,4,1024]{2,1,0:T(4,128)S(1)}, f32[2,4,1024]{2,1,0:T(4,128)S(1)}, u32[]{:S(2)}, u32[]{:S(2)}) collective-permute-start(f32[2,4,1024]{2,1,0:T(4,128)S(1)} %slice.187), channel_id=1, source_target_pairs={{16,0},{32,16},{48,32},{64,48},{80,64},{96,80},{112,96},{17,1},{33... | collective-permute-start | bytes 98312 | tf_op jit(solution)/shard_map/ppermute | solution.py:21
  63.6 19.7 %collective-permute-start = (bf16[1,4,16,256]{3,2,1,0:T(8,128)(2,1)S(1)}, bf16[1,4,16,256]{3,2,1,0:T(8,128)(2,1)S(1)}, u32[]{:S(2)}, u32[]{:S(2)}) collective-permute-start(bf16[1,4,16,256]{3,2,1,0:T(8,128)(2,1)S(1)} %get-tuple-element.34), channel_id=1, source_target_pairs={{0,16},{16,32},{32,48},{48,64},{64,80},{80,96},{96,112},{1,17},{17... | collective-permute-start | bytes 98312 | tf_op jit(solution)/shard_map/ppermute | solution.py:19
  65.6 37.0 %collective-permute-start.1 = (bf16[1,4,16,256]{3,2,1,0:T(8,128)(2,1)S(1)}, bf16[1,4,16,256]{3,2,1,0:T(8,128)(2,1)S(1)}, u32[]{:S(2)}, u32[]{:S(2)}) collective-permute-start(bf16[1,4,16,256]{3,2,1,0:T(8,128)(2,1)S(1)} %get-tuple-element.33), channel_id=1, source_target_pairs={{16,0},{32,16},{48,32},{64,48},{80,64},{96,80},{112,96},{17,1},{33... | collective-permute-start | bytes 98312 | tf_op jit(solution)/shard_map/ppermute | solution.py:21
  69.2 16.8 %collective-permute-start.26 = (f32[5,1024]{1,0:T(8,128)S(1)}, f32[5,1024]{1,0:T(8,128)S(1)}, u32[]{:S(2)}, u32[]{:S(2)}) collective-permute-start(f32[5,1024]{1,0:T(8,128)S(1)} %stack.85), channel_id=1, source_target_pairs={{0,4},{1,5},{2,6},{3,7},{4,8},{5,9},{6,10},{7,11},{8,12},{9,13},{1... | collective-permute-start | bytes 61448 | tf_op jit(solution)/shard_map/ppermute | solution.py:31
  74.8 14.0 %collective-permute-start.27 = (f32[5,1024]{1,0:T(8,128)S(1)}, f32[5,1024]{1,0:T(8,128)S(1)}, u32[]{:S(2)}, u32[]{:S(2)}) collective-permute-start(f32[5,1024]{1,0:T(8,128)S(1)} %stack.85), channel_id=1, source_target_pairs={{0,2},{1,3},{2,4},{3,5},{4,6},{5,7},{6,8},{7,9},{8,10},{9,11},{10,... | collective-permute-start | bytes 61448 | tf_op jit(solution)/shard_map/ppermute | solution.py:31
  80.0 14.1 %collective-permute-start.28 = (f32[5,1024]{1,0:T(8,128)S(1)}, f32[5,1024]{1,0:T(8,128)S(1)}, u32[]{:S(2)}, u32[]{:S(2)}) collective-permute-start(f32[5,1024]{1,0:T(8,128)S(1)} %stack.85), channel_id=1, source_target_pairs={{2,0},{3,1},{4,2},{5,3},{6,4},{7,5},{8,6},{9,7},{10,8},{11,9},{12,... | collective-permute-start | bytes 61448 | tf_op jit(solution)/shard_map/ppermute | solution.py:31
  83.3 12.8 %collective-permute-start.29 = (f32[5,1024]{1,0:T(8,128)S(1)}, f32[5,1024]{1,0:T(8,128)S(1)}, u32[]{:S(2)}, u32[]{:S(2)}) collective-permute-start(f32[5,1024]{1,0:T(8,128)S(1)} %stack.85), channel_id=1, source_target_pairs={{4,0},{5,1},{6,2},{7,3},{8,4},{9,5},{10,6},{11,7},{12,8},{13,9},{1... | collective-permute-start | bytes 61448 | tf_op jit(solution)/shard_map/ppermute | solution.py:31
  86.0 22.1 %collective-permute-start.10 = (f32[6,2,1024]{2,1,0:T(2,128)S(1)}, f32[6,2,1024]{2,1,0:T(2,128)S(1)}, u32[]{:S(2)}, u32[]{:S(2)}) collective-permute-start(f32[6,2,1024]{2,1,0:T(2,128)S(1)} %constant_dynamic-update-slice_fusion.6), channel_id=1, source_target_pairs={{0,1},{1,2},{2,3},{3,4},{4,5},{5,6},{6,7},{7,8},{8,9},{9,10},{10,1... | collective-permute-start | bytes 147464 | tf_op jit(solution)/shard_map/ppermute | solution.py:19
  88.8 25.5 %collective-permute-start.11 = (f32[6,2,1024]{2,1,0:T(2,128)S(1)}, f32[6,2,1024]{2,1,0:T(2,128)S(1)}, u32[]{:S(2)}, u32[]{:S(2)}) collective-permute-start(f32[6,2,1024]{2,1,0:T(2,128)S(1)} %constant_dynamic-update-slice_fusion.6), channel_id=1, source_target_pairs={{1,0},{2,1},{3,2},{4,3},{5,4},{6,5},{7,6},{8,7},{9,8},{10,9},{11,1... | collective-permute-start | bytes 147464 | tf_op jit(solution)/shard_map/ppermute | solution.py:21
  94.1 24.8 %collective-permute-start.6 = (f32[8,2,1024]{2,1,0:T(2,128)S(1)}, f32[8,2,1024]{2,1,0:T(2,128)S(1)}, u32[]{:S(2)}, u32[]{:S(2)}) collective-permute-start(f32[8,2,1024]{2,1,0:T(2,128)S(1)} %get-tuple-element.35), channel_id=1, source_target_pairs={{0,1},{1,2},{2,3},{3,4},{4,5},{5,6},{6,7},{7,8},{8,9},{9,10},{10,1... | collective-permute-start | bytes 196616 | tf_op jit(solution)/shard_map/ppermute | solution.py:19
  96.0 27.7 %collective-permute-start.7 = (f32[8,2,1024]{2,1,0:T(2,128)S(1)}, f32[8,2,1024]{2,1,0:T(2,128)}, u32[]{:S(2)}, u32[]{:S(2)}) collective-permute-start(f32[8,2,1024]{2,1,0:T(2,128)S(1)} %get-tuple-element.36), channel_id=1, source_target_pairs={{1,0},{2,1},{3,2},{4,3},{5,4},{6,5},{7,6},{8,7},{9,8},{10,9},{11,1... | collective-permute-start | bytes 196616 | tf_op jit(solution)/shard_map/ppermute | solution.py:21
  104.4 14.3 %collective-permute-start.2 = (bf16[6,1,16,256]{3,2,1,0:T(8,128)(2,1)S(1)}, bf16[6,1,16,256]{3,2,1,0:T(8,128)(2,1)S(1)}, u32[]{:S(2)}, u32[]{:S(2)}) collective-permute-start(bf16[6,1,16,256]{3,2,1,0:T(8,128)(2,1)S(1)} %get-tuple-element.14), channel_id=1, source_target_pairs={{0,1},{1,2},{2,3},{3,4},{4,5},{5,6},{6,7},{7,8},{8,9},{9,10},{10,1... | collective-permute-start | bytes 147464 | tf_op jit(solution)/shard_map/ppermute | solution.py:19
  108.1 10.7 %collective-permute-start.3 = (bf16[6,1,16,256]{3,2,1,0:T(8,128)(2,1)S(1)}, bf16[6,1,16,256]{3,2,1,0:T(8,128)(2,1)S(1)}, u32[]{:S(2)}, u32[]{:S(2)}) collective-permute-start(bf16[6,1,16,256]{3,2,1,0:T(8,128)(2,1)S(1)} %get-tuple-element.15), channel_id=1, source_target_pairs={{1,0},{2,1},{3,2},{4,3},{5,4},{6,5},{7,6},{8,7},{9,8},{10,9},{11,1... | collective-permute-start | bytes 147464 | tf_op jit(solution)/shard_map/ppermute | solution.py:21
  (3 other events, 35.2 us)
where the time goes:
time: 147 us; the launch traced here: 145 us
  starting transfers between devices  93.5 us (64%)
  matrix products  29 us (20%)
  local copies, waits for them, and re-layouts  14 us (10%)
  other arithmetic  6.7 us (5%)
    ppermute x16, starting transfers between devices, shifted(): return lax.ppermute(block, axis, route)  53.6 us
    ppermute x6, starting transfers between devices, padded_2(): lax.ppermute(head, axis, [((i + 1) % count, i) for i in range(ends)])  25.2 us
    ppermute x6, starting transfers between devices, padded_2(): lax.ppermute(tail, axis, [(i, (i + 1) % count) for i in range(ends)])  12.9 us
    dot_general x2, matrix products, couple_padded(): jnp.einsum('ijkmn,ijkrn->ijrm', coupling, chosen, precision=HIGHEST_PRECI...  11.8 us
    broadcast_in_dim x32, local copies, waits for them, and re-layouts, select_codes(): jnp.where(marks, piece[:, :, None], jnp.zeros((), padded.dtype))  9.71 us
    dot_general x1, matrix products, on_device(): jnp.einsum('ijkab,ijkrb->ijra', near_blocks, neighbours, preferred_elemen...  6.42 us
    eq x3, other arithmetic, select_codes(): marks = (codes == code).reshape(codes.shape + (1,) * len(trailing))  3.37 us
    concatenate x5, other arithmetic, padded_2(): jnp.concatenate([lax.ppermute(tail, axis, [(i, (i + 1) % count) for i in...  3.2 us
  transfers between devices with their start and end apart: 30, of which 2 were waited for; matrix products, arithmetic and copies ran while one was open for 15% of the time, Pallas kernels for 0%

commit v1 on v0

v1 whole, which is shorter than its diff:
```python
import jax
import jax.numpy as jnp
from jax import lax
from jax.experimental import pallas as pl
from jax.experimental.pallas import tpu as pltpu
from jax.sharding import PartitionSpec as P

BF16 = jnp.bfloat16
F32 = jnp.float32
MESH = pl.DeviceIdType.MESH

BESIDE = tuple((u, v) for u in (-1, 0, 1) for v in (-1, 0, 1) if (u, v) != (0, 0))
RING = tuple((u, v) for u in range(-2, 3) for v in range(-2, 3) if max(abs(u), abs(v)) == 2)
PAIRS = ((0, 1), (1, 0), (1, 1))


def span(step, count, width, halo):
    if step == 0:
        return pl.ds(width, count)
    if halo:
        return pl.ds(0, width) if step < 0 else pl.ds(width + count, width)
    return pl.ds(width, width) if step < 0 else pl.ds(count, width)


def folded(total):
    return total + pltpu.roll(total, 64, 1)


def halves(value):
    lane = lax.broadcasted_iota(jnp.int32, value.shape, 1)
    high = value.astype(BF16).astype(F32)
    low = value - high
    first = lane < 64
    return jnp.where(first, high, low).astype(BF16), jnp.where(first, low, high).astype(BF16)


def split_rows(matrix):
    high = matrix.astype(BF16)
    low = (matrix - high.astype(F32)).astype(BF16)
    return jnp.concatenate([high, low], axis=0)


def doubled(matrix):
    return split_rows(jnp.concatenate([matrix, matrix], axis=1))


def times(x, w):
    return lax.dot_general(x, w, (((1,), (0,)), ((), ())), preferred_element_type=F32)


def times_t(x, w):
    return lax.dot_general(x, w, (((1,), (1,)), ((), ())), preferred_element_type=F32)


def kernel(
    sources, near_codes, near_blocks, basis, one, two, three, c_zero, k_zero, c_one, k_one,
    c_two, k_two, c_three, k_three, out,
    s_buf, n_buf, b_buf, t1_buf, t2_buf, t3_buf, c0_buf, c1_buf, c2_buf, c3_buf,
    bs_buf, w1_buf, w2_buf, w3_buf, p0, p1, p2, p3, own2, own3, part, swap0, swap1,
    a0_buf, x1_buf, o_buf,
    load_sem, near_sem, zero_sem, out_sem,
    s_send, s_recv, p0_send, p0_recv, p1_send, p1_recv, p2_send, p2_recv, p3_send, p3_recv,
    g_send, g_recv,
):
    px, py = lax.axis_index("px"), lax.axis_index("py")
    nx, ny = lax.axis_size("px"), lax.axis_size("py")
    row3, col3 = lax.div(px, 2), lax.div(py, 2)

    def valid(u, v):
        return (px + u >= 0) & (px + u < nx) & (py + v >= 0) & (py + v < ny)

    loads = [
        pltpu.make_async_copy(sources, s_buf.at[pl.ds(1, 4), pl.ds(1, 4)], load_sem.at[0]),
        pltpu.make_async_copy(basis, b_buf, load_sem.at[1]),
        pltpu.make_async_copy(one, t1_buf, load_sem.at[2]),
        pltpu.make_async_copy(two, t2_buf, load_sem.at[3]),
        pltpu.make_async_copy(three, t3_buf, load_sem.at[4]),
        pltpu.make_async_copy(c_three.at[row3, col3], c3_buf, load_sem.at[5]),
        pltpu.make_async_copy(c_two, c2_buf, load_sem.at[6]),
        pltpu.make_async_copy(c_one, c1_buf, load_sem.at[7]),
    ]

    def near_load(i, j):
        return pltpu.make_async_copy(near_blocks.at[i, j], n_buf.at[i, j], near_sem.at[i, j])

    def zero_load(i):
        return pltpu.make_async_copy(c_zero.at[i], c0_buf.at[i], zero_sem.at[i])

    for load in loads[:5]:
        load.start()
    for i in range(2):
        for j in range(4):
            near_load(i, j).start()
    for load in loads[5:]:
        load.start()
    for i in range(2, 4):
        for j in range(4):
            near_load(i, j).start()
    for i in range(4):
        zero_load(i).start()

    for buf, n, w in ((s_buf, 4, 1), (p0, 4, 2), (p1, 2, 2)):
        for u, v in BESIDE:
            rows, cols = span(u, n, w, True), span(v, n, w, True)
            shape = (rows.size, cols.size) + buf.shape[2:]
            buf[rows, cols] = jnp.zeros(shape, BF16)
    p2[...] = jnp.zeros(p2.shape, BF16)
    p3[...] = jnp.zeros(p3.shape, BF16)

    barrier = pltpu.get_barrier_semaphore()
    partners = BESIDE + RING + tuple((2 * u, 2 * v) for u, v in RING)
    expected = 0
    for u, v in partners:
        ok = valid(u, v)
        expected = expected + ok.astype(jnp.int32)

        @pl.when(ok)
        def _(u=u, v=v):
            pl.semaphore_signal(barrier, inc=1, device_id=(px + u, py + v), device_id_type=MESH)

    def halo_copy(buf, n, w, send, recv, d):
        u, v = BESIDE[d]
        return pltpu.make_async_remote_copy(
            src_ref=buf.at[span(u, n, w, False), span(v, n, w, False)],
            dst_ref=buf.at[span(-u, n, w, True), span(-v, n, w, True)],
            send_sem=send.at[d], recv_sem=recv.at[d],
            device_id=(px + u, py + v), device_id_type=MESH,
        )

    def ring_copy(own, buf, send, recv, d, stride):
        u, v = RING[d]
        return pltpu.make_async_remote_copy(
            src_ref=own, dst_ref=buf.at[2 - u, 2 - v], send_sem=send.at[d], recv_sem=recv.at[d],
            device_id=(px + stride * u, py + stride * v), device_id_type=MESH,
        )

    def pair_copy(d):
        a, b = PAIRS[d]
        x = px + a * (1 - 2 * lax.rem(px, 2))
        y = py + b * (1 - 2 * lax.rem(py, 2))
        return pltpu.make_async_remote_copy(
            src_ref=part.at[0], dst_ref=part.at[d + 1], send_sem=g_send.at[d],
            recv_sem=g_recv.at[d], device_id=(x, y), device_id_type=MESH,
        )

    halos = {
        "s": (s_buf, 4, 1, s_send, s_recv),
        "0": (p0, 4, 2, p0_send, p0_recv),
        "1": (p1, 2, 2, p1_send, p1_recv),
    }
    rings = {"2": (own2, p2, p2_send, p2_recv, 1), "3": (own3, p3, p3_send, p3_recv, 2)}

    def halo_do(name, act, back):
        buf, n, w, send, recv = halos[name]
        for d, (u, v) in enumerate(BESIDE):

            @pl.when(valid(-u, -v) if back else valid(u, v))
            def _(d=d):
                act(halo_copy(buf, n, w, send, recv, d))

    def ring_do(name, act, back):
        own, buf, send, recv, stride = rings[name]
        for d, (u, v) in enumerate(RING):
            u, v = stride * u, stride * v

            @pl.when(valid(-u, -v) if back else valid(u, v))
            def _(d=d):
                act(ring_copy(own, buf, send, recv, d, stride))

    start = lambda copy: copy.start()
    arrived = lambda copy: copy.wait_recv()
    left = lambda copy: copy.wait_send()

    loads[0].wait()
    loads[1].wait()

    def panel_row(i, carry):
        for j in range(4):
            split = split_rows(b_buf[i, j])
            bs_buf[i, j] = split
            value = folded(times_t(s_buf[i + 1, j + 1], split))
            cat, swapped = halves(value)
            p0[i + 2, j + 2] = cat
            swap0[i, j] = swapped
        return carry

    lax.fori_loop(0, 4, panel_row, 0)
    pl.semaphore_wait(barrier, expected)
    halo_do("s", start, False)
    halo_do("0", start, False)

    loads[2].wait()
    loads[3].wait()
    loads[4].wait()
    for i in range(2):
        for j in range(2):
            total = jnp.zeros((32, 128), F32)
            for a in range(2):
                for b in range(2):
                    r, c = 2 * i + a, 2 * j + b
                    w = doubled(t1_buf[r, c])
                    w1_buf[r, c] = w
                    x = jnp.concatenate([p0[r + 2, c + 2], swap0[r, c]], axis=0)
                    total = total + times(x, w)
            cat, swapped = halves(total[:16] + total[16:])
            p1[i + 2, j + 2] = cat
            swap1[i, j] = swapped
    halo_do("1", start, False)
    total = jnp.zeros((32, 128), F32)
    for i in range(2):
        for j in range(2):
            w = doubled(t2_buf[i, j])
            w2_buf[i, j] = w
            x = jnp.concatenate([p1[i + 2, j + 2], swap1[i, j]], axis=0)
            total = total + times(x, w)
    cat, swapped = halves(total[:16] + total[16:])
    own2[...] = cat
    w = doubled(t3_buf[0, 0])
    w3_buf[...] = w
    total = times(jnp.concatenate([cat, swapped], axis=0), w)
    cat, _ = halves(total[:16] + total[16:])
    own3[...] = cat
    ring_do("3", start, False)
    ring_do("2", start, False)

    halo_do("s", arrived, True)

    def near_row(i, carry):
        for j in range(4):
            near_load(i, j).wait()
            total = jnp.zeros((16, 256), F32)
            for k in range(5):
                code = near_codes[i, j, k]
                u = lax.shift_right_logical(code * 11, 5)
                x = s_buf[i + u, j + code - 3 * u]
                total = total + times_t(x, n_buf[i, j, k])
            o_buf[i, j] = total
        return carry

    lax.fori_loop(0, 2, near_row, 0)

    def coupled(matrices, codes, read):
        total = jnp.zeros((16, 128), F32)
        for k in range(8):
            code = codes(k)
            u = lax.shift_right_logical(code * 13, 6)
            total = total + times_t(read(u, code - 5 * u), doubled(matrices(k)))
        return total

    ring_do("3", arrived, True)
    loads[5].wait()
    total = coupled(
        lambda k: c3_buf[k], lambda k: k_three[row3, col3, k], lambda u, v: p3[u, v]
    )
    cat, _ = halves(folded(total))
    part[0] = cat
    for d in range(3):
        pair_copy(d).start()

    lax.fori_loop(2, 4, near_row, 0)

    ring_do("2", arrived, True)
    loads[6].wait()
    field = coupled(lambda k: c2_buf[0, 0, k], lambda k: k_two[0, 0, k], lambda u, v: p2[u, v])
    halo_do("1", arrived, True)
    loads[7].wait()
    ones = []
    for i in range(2):
        for j in range(2):
            ones.append(
                coupled(
                    lambda k: c1_buf[i, j, k],
                    lambda k: k_one[i, j, k],
                    lambda u, v: p1[i + u, j + v],
                )
            )
    halo_do("0", arrived, True)

    def zero_row(i, carry):
        zero_load(i).wait()
        for j in range(4):
            a0_buf[i, j] = coupled(
                lambda k: c0_buf[i, j, k],
                lambda k: k_zero[i, j, k],
                lambda u, v: p0[i + u, j + v],
            )
        return carry

    lax.fori_loop(0, 4, zero_row, 0)

    for d in range(3):
        pair_copy(d).wait_recv()
    w = w3_buf[...]
    for d in range(4):
        field = field + times_t(part[d], w)
    x2, _ = halves(folded(field))
    for i in range(2):
        for j in range(2):
            total = ones[2 * i + j] + times_t(x2, w2_buf[i, j])
            x1_buf[i, j], _ = halves(folded(total))

    def out_copy(i):
        return pltpu.make_async_copy(o_buf.at[i], out.at[i], out_sem.at[i])

    def far_row(i, carry):
        for j in range(4):
            x1 = x1_buf[lax.div(i, 2), j // 2]
            total = a0_buf[i, j] + times_t(x1, w1_buf[i, j])
            cat, swapped = halves(folded(total))
            far = times(jnp.concatenate([cat, swapped], axis=0), bs_buf[i, j])
            o_buf[i, j] = o_buf[i, j] + (far[:16] + far[16:])
        out_copy(i).start()
        return carry

    lax.fori_loop(0, 4, far_row, 0)

    halo_do("s", left, False)
    halo_do("0", left, False)
    halo_do("1", left, False)
    ring_do("2", left, False)
    ring_do("3", left, False)
    for d in range(3):
        pair_copy(d).wait_send()
    for i in range(4):
        out_copy(i).wait()


def on_device(*args):
    smem = {1, 8, 10, 12, 14}
    dma = pltpu.SemaphoreType.DMA
    vmem = pltpu.VMEM
    return pl.pallas_call(
        kernel,
        out_shape=jax.ShapeDtypeStruct((4, 4, 16, 256), F32),
        in_specs=[
            pl.BlockSpec(memory_space=pltpu.SMEM if at in smem else pl.ANY)
            for at in range(len(args))
        ],
        out_specs=pl.BlockSpec(memory_space=pl.ANY),
        scratch_shapes=[
            vmem((6, 6, 16, 256), BF16),
            vmem((4, 4, 5, 256, 256), BF16),
            vmem((4, 4, 64, 256), F32),
            vmem((4, 4, 64, 64), F32),
            vmem((2, 2, 64, 64), F32),
            vmem((1, 1, 64, 64), F32),
            vmem((4, 4, 8, 64, 64), F32),
            vmem((2, 2, 8, 64, 64), F32),
            vmem((1, 1, 8, 64, 64), F32),
            vmem((8, 64, 64), F32),
            vmem((4, 4, 128, 256), BF16),
            vmem((4, 4, 128, 128), BF16),
            vmem((2, 2, 128, 128), BF16),
            vmem((128, 128), BF16),
            vmem((8, 8, 16, 128), BF16),
            vmem((6, 6, 16, 128), BF16),
            vmem((5, 5, 16, 128), BF16),
            vmem((5, 5, 16, 128), BF16),
            vmem((16, 128), BF16),
            vmem((16, 128), BF16),
            vmem((4, 16, 128), BF16),
            vmem((4, 4, 16, 128), BF16),
            vmem((2, 2, 16, 128), BF16),
            vmem((4, 4, 16, 128), F32),
            vmem((2, 2, 16, 128), BF16),
            vmem((4, 4, 16, 256), F32),
            dma((8,)),
            dma((4, 4)),
            dma((4,)),
            dma((4,)),
        ]
        + [dma((8,))] * 6
        + [dma((16,))] * 4
        + [dma((3,))] * 2,
        compiler_params=pltpu.CompilerParams(
            collective_id=0, has_side_effects=True, vmem_limit_bytes=48 * 1024 * 1024
        ),
        name="patches",
    )(*args)


def solution(mesh):
    grid = P("px", "py")
    placed = (grid,) * 13 + (P(), P())
    return jax.shard_map(
        on_device, mesh=mesh, in_specs=placed, out_specs=grid, check_vma=False
    )
```

time: 147 us -> 43.3 us (0.29)
  the two profiles are of different devices: /device:TPU:100 before, /device:TPU:7 now
where the time goes in v1:
time: 43.3 us; the launch traced here: 42.7 us
  Pallas kernels  31.6 us (73%)
  local copies, waits for them, and re-layouts  11.2 us (26%)
    pallas_call x1, Pallas kernels, on_device(): pl.pallas_call(kernel, out_shape=jax.ShapeDtypeStruct((4, 4, 16, 256), F3...  31.6 us
    unnamed x25, local copies, waits for them, and re-layouts  11.2 us

profile of v1, /device:TPU:7, one launch (start us, length us, event | category | flops | bytes accessed | tf_op | source)
XLA Modules:
  0.0 42.7 jit_solution(4840148212947110553)
XLA Ops:
  0.0 0.0 copy-start
  0.0 1.2 %copy-done = f32[4,4,64,256]{3,2,1,0:T(8,128)S(1)} copy-done((f32[4,4,64,256]{3,2,1,0:T(8,128)S(1)}, f32[4,4,64,256]{3,2,1,0:T(8,128)}, u32[]{:S(2)}) %copy-start) | copy-done | bytes 1048600
  1.2 0.0 copy-start.1
  1.2 1.2 %copy-done.1 = f32[2,2,8,64,64]{4,3,2,1,0:T(8,128)S(1)} copy-done((f32[2,2,8,64,64]{4,3,2,1,0:T(8,128)S(1)}, f32[2,2,8,64,64]{4,3,2,1,0:T(8,128)}, u32[]{:S(2)}) %copy-start.1) | copy-done | bytes 524312
  2.5 0.0 copy-start.2
  2.5 1.0 %copy-done.2 = f32[4,4,64,64]{3,2,1,0:T(8,128)S(1)} copy-done((f32[4,4,64,64]{3,2,1,0:T(8,128)S(1)}, f32[4,4,64,64]{3,2,1,0:T(8,128)}, u32[]{:S(2)}) %copy-start.2) | copy-done | bytes 262168
  3.5 0.0 copy-start.3
  3.5 0.9 %copy-done.3 = f32[1,1,8,64,64]{4,3,2,1,0:T(8,128)S(1)} copy-done((f32[1,1,8,64,64]{4,3,2,1,0:T(8,128)S(1)}, f32[1,1,8,64,64]{4,3,2,1,0:T(8,128)}, u32[]{:S(2)}) %copy-start.3) | copy-done | bytes 131096
  4.4 0.0 copy-start.4
  4.4 0.9 %copy-done.4 = bf16[4,4,16,256]{3,2,1,0:T(8,128)(2,1)S(1)} copy-done((bf16[4,4,16,256]{3,2,1,0:T(8,128)(2,1)S(1)}, bf16[4,4,16,256]{3,2,1,0:T(8,128)(2,1)}, u32[]{:S(2)}) %copy-start.4) | copy-done | bytes 131096
  5.3 0.0 copy-start.5
  5.4 0.9 %copy-done.5 = f32[2,2,64,64]{3,2,1,0:T(8,128)S(1)} copy-done((f32[2,2,64,64]{3,2,1,0:T(8,128)S(1)}, f32[2,2,64,64]{3,2,1,0:T(8,128)}, u32[]{:S(2)}) %copy-start.5) | copy-done | bytes 65560
  6.3 0.0 copy-start.6
  6.3 0.8 %copy-done.6 = f32[1,1,64,64]{3,2,1,0:T(8,128)S(1)} copy-done((f32[1,1,64,64]{3,2,1,0:T(8,128)S(1)}, f32[1,1,64,64]{3,2,1,0:T(8,128)}, u32[]{:S(2)}) %copy-start.6) | copy-done | bytes 16408
  7.0 0.0 copy-start.7
  7.0 0.7 %copy-done.7 = s32[4,8,8]{2,1,0:T(8,128)S(1)} copy-done((s32[4,8,8]{2,1,0:T(8,128)S(1)}, s32[4,8,8]{2,1,0:T(8,128)}, u32[]{:S(2)}) %copy-start.7) | copy-done | bytes 1048
  7.7 0.0 copy-start.8
  7.7 0.7 %copy-done.8 = s32[4,4,5]{2,1,0:T(4,128)S(1)} copy-done((s32[4,4,5]{2,1,0:T(4,128)S(1)}, s32[4,4,5]{2,1,0:T(4,128)}, u32[]{:S(2)}) %copy-start.8) | copy-done | bytes 344
  8.4 0.0 copy-start.9
  8.4 0.7 %copy-done.9 = s32[4,4,8]{2,1,0:T(4,128)S(1)} copy-done((s32[4,4,8]{2,1,0:T(4,128)S(1)}, s32[4,4,8]{2,1,0:T(4,128)}, u32[]{:S(2)}) %copy-start.9) | copy-done | bytes 536
  9.1 0.0 copy-start.10
  9.1 0.7 %copy-done.10 = s32[2,2,8]{2,1,0:T(2,128)S(1)} copy-done((s32[2,2,8]{2,1,0:T(2,128)S(1)}, s32[2,2,8]{2,1,0:T(2,128)}, u32[]{:S(2)}) %copy-start.10) | copy-done | bytes 152
  9.8 0.0 copy-start.11
  9.8 0.7 %copy-done.11 = s32[1,1,8]{2,1,0:T(1,128)S(1)} copy-done((s32[1,1,8]{2,1,0:T(1,128)S(1)}, s32[1,1,8]{2,1,0:T(1,128)}, u32[]{:S(2)}) %copy-start.11) | copy-done | bytes 56
  10.5 31.6 %patches.1 = f32[4,4,16,256]{3,2,1,0:T(8,128)S(1)} custom-call(bf16[4,4,16,256]{3,2,1,0:T(8,128)(2,1)S(1)} %copy-done.4, s32[4,4,5]{2,1,0:T(4,128)S(1)} %copy-done.8, bf16[4,4,5,256,256]{4,3,2,1,0:T(8,128)(2,1)} %near_blocks.1, f32[4,4,64,256]{3,2,1,0:T(8,128)S(1)} %copy-done, f32[4,4,64,64]{3,2,1,0:T(8,128)S(1)} %copy-done.2, ...), custom_call_target="tpu_custom_call" | custom-call | tf_op jit(solution)/shard_map/patches/pallas_call | solution.py:332
  42.0 0.7 %copy.17 = f32[4,4,16,256]{3,2,1,0:T(8,128)} copy(f32[4,4,16,256]{3,2,1,0:T(8,128)S(1)} %patches.1) | data formatting | bytes 524288
Async XLA Ops:
  0.0 1.2 %copy-start = (f32[4,4,64,256]{3,2,1,0:T(8,128)S(1)}, f32[4,4,64,256]{3,2,1,0:T(8,128)}, u32[]{:S(2)}) copy-start(f32[4,4,64,256]{3,2,1,0:T(8,128)} %basis.1) | copy-start | bytes 3145732
  1.2 1.2 %copy-start.1 = (f32[2,2,8,64,64]{4,3,2,1,0:T(8,128)S(1)}, f32[2,2,8,64,64]{4,3,2,1,0:T(8,128)}, u32[]{:S(2)}) copy-start(f32[2,2,8,64,64]{4,3,2,1,0:T(8,128)} %c_one.1) | copy-start | bytes 1572868
  2.5 1.0 %copy-start.2 = (f32[4,4,64,64]{3,2,1,0:T(8,128)S(1)}, f32[4,4,64,64]{3,2,1,0:T(8,128)}, u32[]{:S(2)}) copy-start(f32[4,4,64,64]{3,2,1,0:T(8,128)} %one.1) | copy-start | bytes 786436
  3.5 0.9 %copy-start.3 = (f32[1,1,8,64,64]{4,3,2,1,0:T(8,128)S(1)}, f32[1,1,8,64,64]{4,3,2,1,0:T(8,128)}, u32[]{:S(2)}) copy-start(f32[1,1,8,64,64]{4,3,2,1,0:T(8,128)} %c_two.1) | copy-start | bytes 393220
  4.4 0.9 %copy-start.4 = (bf16[4,4,16,256]{3,2,1,0:T(8,128)(2,1)S(1)}, bf16[4,4,16,256]{3,2,1,0:T(8,128)(2,1)}, u32[]{:S(2)}) copy-start(bf16[4,4,16,256]{3,2,1,0:T(8,128)(2,1)} %sources.1) | copy-start | bytes 393220
  5.3 0.9 %copy-start.5 = (f32[2,2,64,64]{3,2,1,0:T(8,128)S(1)}, f32[2,2,64,64]{3,2,1,0:T(8,128)}, u32[]{:S(2)}) copy-start(f32[2,2,64,64]{3,2,1,0:T(8,128)} %two.1) | copy-start | bytes 196612
  6.3 0.8 %copy-start.6 = (f32[1,1,64,64]{3,2,1,0:T(8,128)S(1)}, f32[1,1,64,64]{3,2,1,0:T(8,128)}, u32[]{:S(2)}) copy-start(f32[1,1,64,64]{3,2,1,0:T(8,128)} %three.1) | copy-start | bytes 49156
  7.0 0.7 %copy-start.7 = (s32[4,8,8]{2,1,0:T(8,128)S(1)}, s32[4,8,8]{2,1,0:T(8,128)}, u32[]{:S(2)}) copy-start(s32[4,8,8]{2,1,0:T(8,128)} %k_three.1) | copy-start | bytes 3076
  7.7 0.7 %copy-start.8 = (s32[4,4,5]{2,1,0:T(4,128)S(1)}, s32[4,4,5]{2,1,0:T(4,128)}, u32[]{:S(2)}) copy-start(s32[4,4,5]{2,1,0:T(4,128)} %near_codes.1) | copy-start | bytes 964
  8.4 0.7 %copy-start.9 = (s32[4,4,8]{2,1,0:T(4,128)S(1)}, s32[4,4,8]{2,1,0:T(4,128)}, u32[]{:S(2)}) copy-start(s32[4,4,8]{2,1,0:T(4,128)} %k_zero.1) | copy-start | bytes 1540
  9.1 0.7 %copy-start.10 = (s32[2,2,8]{2,1,0:T(2,128)S(1)}, s32[2,2,8]{2,1,0:T(2,128)}, u32[]{:S(2)}) copy-start(s32[2,2,8]{2,1,0:T(2,128)} %k_one.1) | copy-start | bytes 388
  9.8 0.7 %copy-start.11 = (s32[1,1,8]{2,1,0:T(1,128)S(1)}, s32[1,1,8]{2,1,0:T(1,128)}, u32[]{:S(2)}) copy-start(s32[1,1,8]{2,1,0:T(1,128)} %k_two.1) | copy-start | bytes 100

commit v2 on v1

--- a/solution.py
+++ b/solution.py
@@ -53,12 +53,13 @@
 
 
 def kernel(
-    sources, near_codes, near_blocks, basis, one, two, three, c_zero, k_zero, c_one, k_one,
-    c_two, k_two, c_three, k_three, out,
+    sources, h_near, near_blocks, basis, one, two, three, c_zero, h_zero, c_one, h_one,
+    c_two, h_two, c_three, h_three, o_buf,
+    near_codes, k_zero, k_one, k_two, k_three,
     s_buf, n_buf, b_buf, t1_buf, t2_buf, t3_buf, c0_buf, c1_buf, c2_buf, c3_buf,
     bs_buf, w1_buf, w2_buf, w3_buf, p0, p1, p2, p3, own2, own3, part, swap0, swap1,
-    a0_buf, x1_buf, o_buf,
-    load_sem, near_sem, zero_sem, out_sem,
+    a0_buf, x1_buf,
+    load_sem, near_sem, zero_sem, code_sem,
     s_send, s_recv, p0_send, p0_recv, p1_send, p1_recv, p2_send, p2_recv, p3_send, p3_recv,
     g_send, g_recv,
 ):
@@ -86,7 +87,14 @@
     def zero_load(i):
         return pltpu.make_async_copy(c_zero.at[i], c0_buf.at[i], zero_sem.at[i])
 
-    for load in loads[:5]:
+    codes = [
+        pltpu.make_async_copy(h_near, near_codes, code_sem.at[0]),
+        pltpu.make_async_copy(h_zero, k_zero, code_sem.at[1]),
+        pltpu.make_async_copy(h_one, k_one, code_sem.at[2]),
+        pltpu.make_async_copy(h_two, k_two, code_sem.at[3]),
+        pltpu.make_async_copy(h_three, k_three, code_sem.at[4]),
+    ]
+    for load in loads[:5] + codes:
         load.start()
     for i in range(2):
         for j in range(4):
@@ -223,6 +231,8 @@
     ring_do("3", start, False)
     ring_do("2", start, False)
 
+    for load in codes:
+        load.wait()
     halo_do("s", arrived, True)
 
     def near_row(i, carry):
@@ -299,9 +309,6 @@
             total = ones[2 * i + j] + times_t(x2, w2_buf[i, j])
             x1_buf[i, j], _ = halves(folded(total))
 
-    def out_copy(i):
-        return pltpu.make_async_copy(o_buf.at[i], out.at[i], out_sem.at[i])
-
     def far_row(i, carry):
         for j in range(4):
             x1 = x1_buf[lax.div(i, 2), j // 2]
@@ -309,7 +316,6 @@
             cat, swapped = halves(folded(total))
             far = times(jnp.concatenate([cat, swapped], axis=0), bs_buf[i, j])
             o_buf[i, j] = o_buf[i, j] + (far[:16] + far[16:])
-        out_copy(i).start()
         return carry
 
     lax.fori_loop(0, 4, far_row, 0)
@@ -321,23 +327,22 @@
     ring_do("3", left, False)
     for d in range(3):
         pair_copy(d).wait_send()
-    for i in range(4):
-        out_copy(i).wait()
 
 
 def on_device(*args):
-    smem = {1, 8, 10, 12, 14}
     dma = pltpu.SemaphoreType.DMA
     vmem = pltpu.VMEM
     return pl.pallas_call(
         kernel,
         out_shape=jax.ShapeDtypeStruct((4, 4, 16, 256), F32),
-        in_specs=[
-            pl.BlockSpec(memory_space=pltpu.SMEM if at in smem else pl.ANY)
-            for at in range(len(args))
-        ],
-        out_specs=pl.BlockSpec(memory_space=pl.ANY),
+        in_specs=[pl.BlockSpec(memory_space=pltpu.HBM)] * len(args),
+        out_specs=pl.BlockSpec(memory_space=pltpu.VMEM),
         scratch_shapes=[
+            pltpu.SMEM((4, 4, 5), jnp.int32),
+            pltpu.SMEM((4, 4, 8), jnp.int32),
+            pltpu.SMEM((2, 2, 8), jnp.int32),
+            pltpu.SMEM((1, 1, 8), jnp.int32),
+            pltpu.SMEM(args[14].shape, jnp.int32),
             vmem((6, 6, 16, 256), BF16),
             vmem((4, 4, 5, 256, 256), BF16),
             vmem((4, 4, 64, 256), F32),
@@ -363,17 +368,16 @@
             vmem((2, 2, 16, 128), BF16),
             vmem((4, 4, 16, 128), F32),
             vmem((2, 2, 16, 128), BF16),
-            vmem((4, 4, 16, 256), F32),
             dma((8,)),
             dma((4, 4)),
             dma((4,)),
-            dma((4,)),
+            dma((5,)),
         ]
         + [dma((8,))] * 6
         + [dma((16,))] * 4
         + [dma((3,))] * 2,
         compiler_params=pltpu.CompilerParams(
-            collective_id=0, has_side_effects=True, vmem_limit_bytes=48 * 1024 * 1024
+            collective_id=0, has_side_effects=True, vmem_limit_bytes=60 * 1024 * 1024
         ),
         name="patches",
     )(*args)

time: 43.3 us -> 32.5 us (0.75)
  the two profiles are of different devices: /device:TPU:7 before, /device:TPU:6 now
where the time goes in v2:
time: 32.5 us; the launch traced here: 32.4 us
  Pallas kernels  30.7 us (94%)
  local copies, waits for them, and re-layouts  1.67 us (5%)
    pallas_call x1, Pallas kernels, on_device(): pl.pallas_call(kernel, out_shape=jax.ShapeDtypeStruct((4, 4, 16, 256), F3...  30.7 us
    unnamed x1, local copies, waits for them, and re-layouts  1.67 us

profile of v2, /device:TPU:6, one launch (start us, length us, event | category | flops | bytes accessed | tf_op | source)
XLA Modules:
  0.0 32.4 jit_solution(2698110036754523847)
XLA Ops:
  0.0 30.7 %patches.1 = f32[4,4,16,256]{3,2,1,0:T(8,128)} custom-call(bf16[4,4,16,256]{3,2,1,0:T(8,128)(2,1)} %sources.1, s32[4,4,5]{2,1,0:T(4,128)} %h_near.1, bf16[4,4,5,256,256]{4,3,2,1,0:T(8,128)(2,1)} %near_blocks.1, f32[4,4,64,256]{3,2,1,0:T(8,128)} %basis.1, f32[4,4,64,64]{3,2,1,0:T(8,128)} %one.1, f32[2,2,64,64]{3,2,1,0:T(8,128)} %two.1, ...), custom_call_target="tpu_custom_call" | custom-call | tf_op jit(solution)/shard_map/patches/pallas_call | solution.py:335
  30.7 1.7 %copy.17 = f32[4,4,16,256]{3,2,1,0:T(8,128)} copy(f32[4,4,16,256]{3,2,1,0:T(8,128)} %patches.1) | data formatting | bytes 524288

commit v3 on v2

v3 whole, which is shorter than its diff:
```python
import jax
import jax.numpy as jnp
from jax import lax
from jax.experimental import pallas as pl
from jax.experimental.pallas import tpu as pltpu
from jax.sharding import PartitionSpec as P

BF16 = jnp.bfloat16
F32 = jnp.float32
MESH = pl.DeviceIdType.MESH

BESIDE = tuple((u, v) for u in (-1, 0, 1) for v in (-1, 0, 1) if (u, v) != (0, 0))
RING = tuple((u, v) for u in range(-2, 3) for v in range(-2, 3) if max(abs(u), abs(v)) == 2)
PAIRS = ((0, 1), (1, 0), (1, 1))


def span(step, count, width, halo):
    if step == 0:
        return pl.ds(width, count)
    if halo:
        return pl.ds(0, width) if step < 0 else pl.ds(width + count, width)
    return pl.ds(width, width) if step < 0 else pl.ds(count, width)


def edge_of(step, count, width):
    if step == 0:
        return pl.ds(0, count)
    return pl.ds(0, width) if step < 0 else pl.ds(count - width, width)


def folded(total):
    return total + pltpu.roll(total, 64, 1)


def halves(value):
    lane = lax.broadcasted_iota(jnp.int32, value.shape, 1)
    high = value.astype(BF16).astype(F32)
    low = value - high
    first = lane < 64
    return jnp.where(first, high, low).astype(BF16), jnp.where(first, low, high).astype(BF16)


def split_rows(matrix):
    high = matrix.astype(BF16)
    low = (matrix - high.astype(F32)).astype(BF16)
    return jnp.concatenate([high, low], axis=0)


def doubled(matrix):
    return split_rows(jnp.concatenate([matrix, matrix], axis=1))


def times(x, w):
    return lax.dot_general(x, w, (((1,), (0,)), ((), ())), preferred_element_type=F32)


def times_t(x, w):
    return lax.dot_general(x, w, (((1,), (1,)), ((), ())), preferred_element_type=F32)


def kernel(
    sources, h_near, near_blocks, basis, one, two, three, c_zero, h_zero, c_one, h_one,
    c_two, h_two, c_three, h_three, out,
    near_codes, k_zero, k_one, k_two, k_three,
    s_own, s_buf, n_buf, b_buf, t1_buf, t2_buf, t3_buf, c0_buf, c1_buf, c2_buf, c3_buf,
    bs_buf, w1_buf, p0, p1, p2, p3, own2, own3, part, o_buf,
    load_sem, near_sem, zero_sem, code_sem, out_sem,
    s_send, s_recv, p0_send, p0_recv, p1_send, p1_recv, p2_send, p2_recv, p3_send, p3_recv,
    g_send, g_recv,
):
    px, py = lax.axis_index("px"), lax.axis_index("py")
    nx, ny = lax.axis_size("px"), lax.axis_size("py")
    row3, col3 = lax.div(px, 2), lax.div(py, 2)
    blocks = tuple((i, j) for i in range(4) for j in range(4))
    inner = tuple((i, j) for i in (1, 2) for j in (1, 2))
    edge = tuple(block for block in blocks if block not in inner)

    def valid(u, v):
        ok = None
        for at, step, count in ((px, u, nx), (py, v, ny)):
            if step:
                here = at + step < count if step > 0 else at + step >= 0
                ok = here if ok is None else ok & here
        return ok

    loads = [
        pltpu.make_async_copy(sources, s_own, load_sem.at[0]),
        pltpu.make_async_copy(basis, b_buf, load_sem.at[1]),
        pltpu.make_async_copy(one, t1_buf, load_sem.at[2]),
        pltpu.make_async_copy(two, t2_buf, load_sem.at[3]),
        pltpu.make_async_copy(three, t3_buf, load_sem.at[4]),
        pltpu.make_async_copy(c_three.at[row3, col3], c3_buf, load_sem.at[5]),
        pltpu.make_async_copy(c_two, c2_buf, load_sem.at[6]),
        pltpu.make_async_copy(c_one, c1_buf, load_sem.at[7]),
        pltpu.make_async_copy(sources, s_buf.at[pl.ds(1, 4), pl.ds(1, 4)], load_sem.at[8]),
    ]
    pieces = (
        (pl.ds(0, 4), pl.ds(0, 4), pl.ds(0, 1)),
        (pl.ds(1, 2), pl.ds(1, 2), pl.ds(1, 4)),
        (pl.ds(0, 1), pl.ds(0, 4), pl.ds(1, 4)),
        (pl.ds(1, 2), pl.ds(0, 1), pl.ds(1, 4)),
        (pl.ds(1, 2), pl.ds(3, 1), pl.ds(1, 4)),
        (pl.ds(3, 1), pl.ds(0, 4), pl.ds(1, 4)),
    )
    near_loads = [
        pltpu.make_async_copy(near_blocks.at[piece], n_buf.at[piece], near_sem.at[at])
        for at, piece in enumerate(pieces)
    ]
    zero_loads = [
        pltpu.make_async_copy(c_zero.at[i], c0_buf.at[i], zero_sem.at[i]) for i in range(4)
    ]
    codes = [
        pltpu.make_async_copy(h_near, near_codes, code_sem.at[0]),
        pltpu.make_async_copy(h_zero, k_zero, code_sem.at[1]),
        pltpu.make_async_copy(h_one, k_one, code_sem.at[2]),
        pltpu.make_async_copy(h_two, k_two, code_sem.at[3]),
        pltpu.make_async_copy(h_three, k_three, code_sem.at[4]),
    ]
    for load in loads[:5] + codes:
        load.start()

    for buf, n, w in ((s_buf, 4, 1), (p0, 4, 2), (p1, 2, 2)):
        for u, v in BESIDE:
            rows, cols = span(u, n, w, True), span(v, n, w, True)
            shape = (rows.size, cols.size) + buf.shape[2:]
            buf[rows, cols] = jnp.zeros(shape, BF16)
    p2[...] = jnp.zeros(p2.shape, BF16)
    p3[...] = jnp.zeros(p3.shape, BF16)

    barrier = pltpu.get_barrier_semaphore()
    partners = BESIDE + RING + tuple((2 * u, 2 * v) for u, v in RING)
    expected = 0
    for u, v in partners:
        ok = valid(u, v)
        expected = expected + ok.astype(jnp.int32)

        @pl.when(ok)
        def _(u=u, v=v):
            pl.semaphore_signal(barrier, inc=1, device_id=(px + u, py + v), device_id_type=MESH)

    for load in near_loads + loads[5:] + zero_loads:
        load.start()

    def halo_copy(buf, n, w, send, recv, d, own=None):
        u, v = BESIDE[d]
        if own is None:
            src = buf.at[span(u, n, w, False), span(v, n, w, False)]
        else:
            src = own.at[edge_of(u, n, w), edge_of(v, n, w)]
        return pltpu.make_async_remote_copy(
            src_ref=src,
            dst_ref=buf.at[span(-u, n, w, True), span(-v, n, w, True)],
            send_sem=send.at[d], recv_sem=recv.at[d],
            device_id=(px + u, py + v), device_id_type=MESH,
        )

    def ring_copy(own, buf, send, recv, d, stride):
        u, v = RING[d]
        return pltpu.make_async_remote_copy(
            src_ref=own, dst_ref=buf.at[2 - u, 2 - v], send_sem=send.at[d], recv_sem=recv.at[d],
            device_id=(px + stride * u, py + stride * v), device_id_type=MESH,
        )

    def pair_copy(d):
        a, b = PAIRS[d]
        x = px + a * (1 - 2 * lax.rem(px, 2))
        y = py + b * (1 - 2 * lax.rem(py, 2))
        return pltpu.make_async_remote_copy(
            src_ref=part.at[0], dst_ref=part.at[d + 1], send_sem=g_send.at[d],
            recv_sem=g_recv.at[d], device_id=(x, y), device_id_type=MESH,
        )

    halos = {
        "s": (s_buf, 4, 1, s_send, s_recv),
        "0": (p0, 4, 2, p0_send, p0_recv),
        "1": (p1, 2, 2, p1_send, p1_recv),
    }
    rings = {"2": (own2, p2, p2_send, p2_recv, 1), "3": (own3, p3, p3_send, p3_recv, 2)}

    def halo_do(name, act, back):
        buf, n, w, send, recv = halos[name]
        for d, (u, v) in enumerate(BESIDE):

            @pl.when(valid(-u, -v) if back else valid(u, v))
            def _(d=d):
                act(halo_copy(buf, n, w, send, recv, d, s_own if name == "s" else None))

    def ring_do(name, act, back):
        own, buf, send, recv, stride = rings[name]
        for d, (u, v) in enumerate(RING):
            u, v = stride * u, stride * v

            @pl.when(valid(-u, -v) if back else valid(u, v))
            def _(d=d):
                act(ring_copy(own, buf, send, recv, d, stride))

    start = lambda copy: copy.start()
    arrived = lambda copy: copy.wait_recv()
    left = lambda copy: copy.wait_send()

    for load in loads[:5]:
        load.wait()
    totals = {}
    for i, j in blocks:
        split = split_rows(b_buf[i, j])
        bs_buf[i, j] = split
        totals[i, j] = times_t(s_own[i, j], split)
    below = {}
    for i, j in blocks:
        below[i, j] = halves(folded(totals[i, j]))
        p0[i + 2, j + 2] = below[i, j][0]
    above = {}
    for i in range(2):
        for j in range(2):
            total = jnp.zeros((32, 128), F32)
            for a in range(2):
                for b in range(2):
                    r, c = 2 * i + a, 2 * j + b
                    w = doubled(t1_buf[r, c])
                    w1_buf[r, c] = w
                    total = total + times(jnp.concatenate(below[r, c], axis=0), w)
            above[i, j] = halves(total[:16] + total[16:])
            p1[i + 2, j + 2] = above[i, j][0]
    total = jnp.zeros((32, 128), F32)
    for i in range(2):
        for j in range(2):
            total = total + times(jnp.concatenate(above[i, j], axis=0), doubled(t2_buf[i, j]))
    pair = halves(total[:16] + total[16:])
    own2[...] = pair[0]
    total = times(jnp.concatenate(pair, axis=0), doubled(t3_buf[0, 0]))
    own3[...] = halves(total[:16] + total[16:])[0]

    pl.semaphore_wait(barrier, expected)
    halo_do("s", start, False)
    ring_do("3", start, False)
    ring_do("2", start, False)
    halo_do("1", start, False)
    halo_do("0", start, False)

    def near_product(i, j, k, buf, shift):
        code = near_codes[i, j, k]
        u = lax.shift_right_logical(code * 11, 5)
        x = buf[i + u - shift, j + code - 3 * u - shift]
        return times_t(x, n_buf[i, j, k])

    for load in codes:
        load.wait()
    near_loads[0].wait()
    near_loads[1].wait()
    for i, j in blocks:
        total = times_t(s_own[i, j], n_buf[i, j, 0])
        if (i, j) in inner:
            for k in range(1, 5):
                total = total + near_product(i, j, k, s_own, 1)
        o_buf[i, j] = total

    loads[8].wait()
    halo_do("s", arrived, True)

    def near_edge(some):
        for i, j in some:
            total = o_buf[i, j]
            for k in range(1, 5):
                total = total + near_product(i, j, k, s_buf, 0)
            o_buf[i, j] = total

    def coupled(matrices, codes, read, total=None):
        for k in range(0, 8, 2):
            xs, ws = [], []
            for q in (k, k + 1):
                code = codes(q)
                u = lax.shift_right_logical(code * 13, 6)
                xs.append(read(u, code - 5 * u))
                ws.append(doubled(matrices(q)))
            term = times_t(jnp.concatenate(xs, axis=1), jnp.concatenate(ws, axis=1))
            total = term if total is None else total + term
        return total

    ring_do("3", arrived, True)
    loads[5].wait()
    for load in near_loads[2:4]:
        load.wait()
    total = coupled(
        lambda k: c3_buf[k], lambda k: k_three[row3, col3, k], lambda u, v: p3[u, v]
    )
    part[0] = halves(folded(total))[0]
    near_edge(edge[:4] + ((1, 0), (2, 0)))
    for d in range(3):
        pair_copy(d).start()
    for load in near_loads[4:]:
        load.wait()
    near_edge(((1, 3), (2, 3)) + edge[8:])

    ring_do("2", arrived, True)
    halo_do("1", arrived, True)
    halo_do("0", arrived, True)
    for load in loads[6:8] + zero_loads:
        load.wait()
    field = coupled(lambda k: c2_buf[0, 0, k], lambda k: k_two[0, 0, k], lambda u, v: p2[u, v])
    ones = {}
    for i in range(2):
        for j in range(2):
            ones[i, j] = coupled(
                lambda k: c1_buf[i, j, k],
                lambda k: k_one[i, j, k],
                lambda u, v: p1[i + u, j + v],
            )
    zeros = {}
    for i, j in blocks:
        zeros[i, j] = coupled(
            lambda k: c0_buf[i, j, k],
            lambda k: k_zero[i, j, k],
            lambda u, v: p0[i + u, j + v],
        )

    for d in range(3):
        pair_copy(d).wait_recv()
    w = doubled(t3_buf[0, 0])
    for d in range(4):
        field = field + times_t(part[d], w)
    x2 = halves(folded(field))[0]
    x1 = {}
    for i in range(2):
        for j in range(2):
            total = ones[i, j] + times_t(x2, doubled(t2_buf[i, j]))
            x1[i, j] = halves(folded(total))[0]
    for i, j in blocks:
        zeros[i, j] = zeros[i, j] + times_t(x1[i // 2, j // 2], w1_buf[i, j])
    outs = [pltpu.make_async_copy(o_buf.at[i], out.at[i], out_sem.at[i]) for i in range(4)]
    for i, j in blocks:
        pair = halves(folded(zeros[i, j]))
        far = times(jnp.concatenate(pair, axis=0), bs_buf[i, j])
        o_buf[i, j] = o_buf[i, j] + (far[:16] + far[16:])
        if j == 3:
            outs[i].start()

    halo_do("s", left, False)
    halo_do("0", left, False)
    halo_do("1", left, False)
    ring_do("2", left, False)
    ring_do("3", left, False)
    for d in range(3):
        pair_copy(d).wait_send()
    for copy in outs:
        copy.wait()


def on_device(*args):
    dma = pltpu.SemaphoreType.DMA
    vmem = pltpu.VMEM
    return pl.pallas_call(
        kernel,
        out_shape=jax.ShapeDtypeStruct((4, 4, 16, 256), F32),
        in_specs=[pl.BlockSpec(memory_space=pltpu.HBM)] * len(args),
        out_specs=pl.BlockSpec(memory_space=pltpu.HBM),
        scratch_shapes=[
            pltpu.SMEM((4, 4, 5), jnp.int32),
            pltpu.SMEM((4, 4, 8), jnp.int32),
            pltpu.SMEM((2, 2, 8), jnp.int32),
            pltpu.SMEM((1, 1, 8), jnp.int32),
            pltpu.SMEM(args[14].shape, jnp.int32),
            vmem((4, 4, 16, 256), BF16),
            vmem((6, 6, 16, 256), BF16),
            vmem((4, 4, 5, 256, 256), BF16),
            vmem((4, 4, 64, 256), F32),
            vmem((4, 4, 64, 64), F32),
            vmem((2, 2, 64, 64), F32),
            vmem((1, 1, 64, 64), F32),
            vmem((4, 4, 8, 64, 64), F32),
            vmem((2, 2, 8, 64, 64), F32),
            vmem((1, 1, 8, 64, 64), F32),
            vmem((8, 64, 64), F32),
            vmem((4, 4, 128, 256), BF16),
            vmem((4, 4, 128, 128), BF16),
            vmem((8, 8, 16, 128), BF16),
            vmem((6, 6, 16, 128), BF16),
            vmem((5, 5, 16, 128), BF16),
            vmem((5, 5, 16, 128), BF16),
            vmem((16, 128), BF16),
            vmem((16, 128), BF16),
            vmem((4, 16, 128), BF16),
            vmem((4, 4, 16, 256), F32),
            dma((9,)),
            dma((6,)),
            dma((4,)),
            dma((5,)),
            dma((4,)),
        ]
        + [dma((8,))] * 6
        + [dma((16,))] * 4
        + [dma((3,))] * 2,
        compiler_params=pltpu.CompilerParams(
            collective_id=0, has_side_effects=True, vmem_limit_bytes=60 * 1024 * 1024
        ),
        name="patches",
    )(*args)


def solution(mesh):
    grid = P("px", "py")
    placed = (grid,) * 13 + (P(), P())
    return jax.shard_map(
        on_device, mesh=mesh, in_specs=placed, out_specs=grid, check_vma=False
    )
```

time: 32.5 us -> 22.2 us (0.68)
  the two profiles are of different devices: /device:TPU:6 before, /device:TPU:1 now
where the time goes in v3:
time: 22.2 us; the launch traced here: 22.1 us
  Pallas kernels  20.4 us (92%)
  local copies, waits for them, and re-layouts  1.67 us (8%)
    pallas_call x1, Pallas kernels, on_device(): pl.pallas_call(kernel, out_shape=jax.ShapeDtypeStruct((4, 4, 16, 256), F3...  20.4 us
    unnamed x1, local copies, waits for them, and re-layouts  1.67 us

profile of v3, /device:TPU:1, one launch (start us, length us, event | category | flops | bytes accessed | tf_op | source)
XLA Modules:
  0.0 22.1 jit_solution(12191202637583907516)
XLA Ops:
  0.0 20.4 %patches.1 = f32[4,4,16,256]{3,2,1,0:T(8,128)} custom-call(bf16[4,4,16,256]{3,2,1,0:T(8,128)(2,1)} %sources.1, s32[4,4,5]{2,1,0:T(4,128)} %h_near.1, bf16[4,4,5,256,256]{4,3,2,1,0:T(8,128)(2,1)} %near_blocks.1, f32[4,4,64,256]{3,2,1,0:T(8,128)} %basis.1, f32[4,4,64,64]{3,2,1,0:T(8,128)} %one.1, f32[2,2,64,64]{3,2,1,0:T(8,128)} %two.1, ...), custom_call_target="tpu_custom_call" | custom-call | tf_op jit(solution)/shard_map/patches/pallas_call | solution.py:351
  20.4 1.7 %copy.17 = f32[4,4,16,256]{3,2,1,0:T(8,128)} copy(f32[4,4,16,256]{3,2,1,0:T(8,128)} %patches.1) | data formatting | bytes 524288

commit v4 on v3

--- a/solution.py
+++ b/solution.py
@@ -64,9 +64,9 @@
     near_codes, k_zero, k_one, k_two, k_three,
     s_own, s_buf, n_buf, b_buf, t1_buf, t2_buf, t3_buf, c0_buf, c1_buf, c2_buf, c3_buf,
     bs_buf, w1_buf, p0, p1, p2, p3, own2, own3, part, o_buf,
+    none, s_none, s_spare, spare0, spare1, spare2, spare3,
     load_sem, near_sem, zero_sem, code_sem, out_sem,
-    s_send, s_recv, p0_send, p0_recv, p1_send, p1_recv, p2_send, p2_recv, p3_send, p3_recv,
-    g_send, g_recv,
+    send_sem, recv_sem,
 ):
     px, py = lax.axis_index("px"), lax.axis_index("py")
     nx, ny = lax.axis_size("px"), lax.axis_size("py")
@@ -107,7 +107,7 @@
         for at, piece in enumerate(pieces)
     ]
     zero_loads = [
-        pltpu.make_async_copy(c_zero.at[i], c0_buf.at[i], zero_sem.at[i]) for i in range(4)
+        pltpu.make_async_copy(c_zero.at[i], c0_buf.at[i], zero_sem) for i in range(4)
     ]
     codes = [
         pltpu.make_async_copy(h_near, near_codes, code_sem.at[0]),
@@ -119,14 +119,6 @@
     for load in loads[:5] + codes:
         load.start()
 
-    for buf, n, w in ((s_buf, 4, 1), (p0, 4, 2), (p1, 2, 2)):
-        for u, v in BESIDE:
-            rows, cols = span(u, n, w, True), span(v, n, w, True)
-            shape = (rows.size, cols.size) + buf.shape[2:]
-            buf[rows, cols] = jnp.zeros(shape, BF16)
-    p2[...] = jnp.zeros(p2.shape, BF16)
-    p3[...] = jnp.zeros(p3.shape, BF16)
-
     barrier = pltpu.get_barrier_semaphore()
     partners = BESIDE + RING + tuple((2 * u, 2 * v) for u, v in RING)
     expected = 0
@@ -138,68 +130,74 @@
         def _(u=u, v=v):
             pl.semaphore_signal(barrier, inc=1, device_id=(px + u, py + v), device_id_type=MESH)
 
-    for load in near_loads + loads[5:] + zero_loads:
+    none[...] = jnp.zeros(none.shape, BF16)
+    s_none[...] = jnp.zeros(s_none.shape, BF16)
+
+    def group_send(u, v, stride, at, src, dst, back, spare, zeros):
+        ok = valid(stride * u, stride * v)
+
+        @pl.when(ok)
+        def _():
+            pltpu.make_async_remote_copy(
+                src_ref=src, dst_ref=dst, send_sem=send_sem.at[at], recv_sem=recv_sem.at[at],
+                device_id=(px + stride * u, py + stride * v), device_id_type=MESH,
+            ).start()
+
+        @pl.when(jnp.logical_not(ok))
+        def _():
+            pltpu.make_async_copy(zeros, back, recv_sem.at[at]).start()
+            pltpu.make_async_copy(zeros, spare, send_sem.at[at]).start()
+
+    def halo_send(buf, n, w, at, spare, zeros, own=None):
+        for u, v in BESIDE:
+            if own is None:
+                src = buf.at[span(u, n, w, False), span(v, n, w, False)]
+            else:
+                src = own.at[edge_of(u, n, w), edge_of(v, n, w)]
+            there = span(-u, n, w, True), span(-v, n, w, True)
+            here = span(u, n, w, True), span(v, n, w, True)
+            nothing = zeros.at[pl.ds(0, here[0].size), pl.ds(0, here[1].size)]
+            group_send(u, v, 1, at, src, buf.at[there], buf.at[here], spare.at[here], nothing)
+
+    def ring_send(own, buf, stride, at, spare):
+        for u, v in RING:
+            here = 2 + u, 2 + v
+            nothing = none.at[0, 0]
+            group_send(
+                u, v, stride, at, own, buf.at[2 - u, 2 - v], buf.at[here], spare.at[here], nothing
+            )
+
+    def pair_send():
+        for d, (a, b) in enumerate(PAIRS):
+            x = px + a * (1 - 2 * lax.rem(px, 2))
+            y = py + b * (1 - 2 * lax.rem(py, 2))
+            pltpu.make_async_remote_copy(
+                src_ref=part.at[0], dst_ref=part.at[d + 1],
+                send_sem=send_sem.at[5], recv_sem=recv_sem.at[5],
+                device_id=(x, y), device_id_type=MESH,
+            ).start()
+
+    sizes = (
+        s_buf.at[pl.ds(0, 5), pl.ds(0, 4)],
+        p0.at[pl.ds(0, 6)],
+        p0.at[pl.ds(0, 4)],
+        p2.at[pl.ds(0, 4), pl.ds(0, 4)],
+        p3.at[pl.ds(0, 4), pl.ds(0, 4)],
+        part.at[pl.ds(1, 3)],
+    )
+
+    def arrived(at):
+        pltpu.make_async_copy(sizes[at], sizes[at], recv_sem.at[at]).wait()
+
+    def left(at):
+        pltpu.make_async_copy(sizes[at], sizes[at], send_sem.at[at]).wait()
+
+    for load in near_loads[:2]:
         load.start()
-
-    def halo_copy(buf, n, w, send, recv, d, own=None):
-        u, v = BESIDE[d]
-        if own is None:
-            src = buf.at[span(u, n, w, False), span(v, n, w, False)]
-        else:
-            src = own.at[edge_of(u, n, w), edge_of(v, n, w)]
-        return pltpu.make_async_remote_copy(
-            src_ref=src,
-            dst_ref=buf.at[span(-u, n, w, True), span(-v, n, w, True)],
-            send_sem=send.at[d], recv_sem=recv.at[d],
-            device_id=(px + u, py + v), device_id_type=MESH,
-        )
-
-    def ring_copy(own, buf, send, recv, d, stride):
-        u, v = RING[d]
-        return pltpu.make_async_remote_copy(
-            src_ref=own, dst_ref=buf.at[2 - u, 2 - v], send_sem=send.at[d], recv_sem=recv.at[d],
-            device_id=(px + stride * u, py + stride * v), device_id_type=MESH,
-        )
-
-    def pair_copy(d):
-        a, b = PAIRS[d]
-        x = px + a * (1 - 2 * lax.rem(px, 2))
-        y = py + b * (1 - 2 * lax.rem(py, 2))
-        return pltpu.make_async_remote_copy(
-            src_ref=part.at[0], dst_ref=part.at[d + 1], send_sem=g_send.at[d],
-            recv_sem=g_recv.at[d], device_id=(x, y), device_id_type=MESH,
-        )
-
-    halos = {
-        "s": (s_buf, 4, 1, s_send, s_recv),
-        "0": (p0, 4, 2, p0_send, p0_recv),
-        "1": (p1, 2, 2, p1_send, p1_recv),
-    }
-    rings = {"2": (own2, p2, p2_send, p2_recv, 1), "3": (own3, p3, p3_send, p3_recv, 2)}
-
-    def halo_do(name, act, back):
-        buf, n, w, send, recv = halos[name]
-        for d, (u, v) in enumerate(BESIDE):
-
-            @pl.when(valid(-u, -v) if back else valid(u, v))
-            def _(d=d):
-                act(halo_copy(buf, n, w, send, recv, d, s_own if name == "s" else None))
-
-    def ring_do(name, act, back):
-        own, buf, send, recv, stride = rings[name]
-        for d, (u, v) in enumerate(RING):
-            u, v = stride * u, stride * v
-
-            @pl.when(valid(-u, -v) if back else valid(u, v))
-            def _(d=d):
-                act(ring_copy(own, buf, send, recv, d, stride))
-
-    start = lambda copy: copy.start()
-    arrived = lambda copy: copy.wait_recv()
-    left = lambda copy: copy.wait_send()
-
-    for load in loads[:5]:
-        load.wait()
+    loads[0].wait()
+    loads[1].wait()
+    for load in near_loads[2:4] + [loads[8], loads[5]]:
+        load.start()
     totals = {}
     for i, j in blocks:
         split = split_rows(b_buf[i, j])
@@ -209,6 +207,8 @@
     for i, j in blocks:
         below[i, j] = halves(folded(totals[i, j]))
         p0[i + 2, j + 2] = below[i, j][0]
+    for load in loads[2:5]:
+        load.wait()
     above = {}
     for i in range(2):
         for j in range(2):
@@ -226,16 +226,18 @@
         for j in range(2):
             total = total + times(jnp.concatenate(above[i, j], axis=0), doubled(t2_buf[i, j]))
     pair = halves(total[:16] + total[16:])
+    for load in near_loads[4:] + loads[6:8]:
+        load.start()
     own2[...] = pair[0]
     total = times(jnp.concatenate(pair, axis=0), doubled(t3_buf[0, 0]))
     own3[...] = halves(total[:16] + total[16:])[0]
 
     pl.semaphore_wait(barrier, expected)
-    halo_do("s", start, False)
-    ring_do("3", start, False)
-    ring_do("2", start, False)
-    halo_do("1", start, False)
-    halo_do("0", start, False)
+    halo_send(s_buf, 4, 1, 0, s_spare, s_none, s_own)
+    ring_send(own3, p3, 2, 4, spare3)
+    ring_send(own2, p2, 1, 3, spare2)
+    halo_send(p1, 2, 2, 2, spare1, none)
+    halo_send(p0, 4, 2, 1, spare0, none)
 
     def near_product(i, j, k, buf, shift):
         code = near_codes[i, j, k]
@@ -254,8 +256,11 @@
                 total = total + near_product(i, j, k, s_own, 1)
         o_buf[i, j] = total
 
+    for load in zero_loads:
+        load.start()
     loads[8].wait()
-    halo_do("s", arrived, True)
+    arrived(0)
+    arrived(4)
 
     def near_edge(some):
         for i, j in some:
@@ -276,7 +281,6 @@
             total = term if total is None else total + term
         return total
 
-    ring_do("3", arrived, True)
     loads[5].wait()
     for load in near_loads[2:4]:
         load.wait()
@@ -285,17 +289,16 @@
     )
     part[0] = halves(folded(total))[0]
     near_edge(edge[:4] + ((1, 0), (2, 0)))
-    for d in range(3):
-        pair_copy(d).start()
+    pair_send()
     for load in near_loads[4:]:
         load.wait()
     near_edge(((1, 3), (2, 3)) + edge[8:])
 
-    ring_do("2", arrived, True)
-    halo_do("1", arrived, True)
-    halo_do("0", arrived, True)
-    for load in loads[6:8] + zero_loads:
+    for at in (3, 2, 1):
+        arrived(at)
+    for load in loads[6:8]:
         load.wait()
+    pltpu.make_async_copy(c_zero, c0_buf, zero_sem).wait()
     field = coupled(lambda k: c2_buf[0, 0, k], lambda k: k_two[0, 0, k], lambda u, v: p2[u, v])
     ones = {}
     for i in range(2):
@@ -313,8 +316,7 @@
             lambda u, v: p0[i + u, j + v],
         )
 
-    for d in range(3):
-        pair_copy(d).wait_recv()
+    arrived(5)
     w = doubled(t3_buf[0, 0])
     for d in range(4):
         field = field + times_t(part[d], w)
@@ -326,7 +328,7 @@
             x1[i, j] = halves(folded(total))[0]
     for i, j in blocks:
         zeros[i, j] = zeros[i, j] + times_t(x1[i // 2, j // 2], w1_buf[i, j])
-    outs = [pltpu.make_async_copy(o_buf.at[i], out.at[i], out_sem.at[i]) for i in range(4)]
+    outs = [pltpu.make_async_copy(o_buf.at[i], out.at[i], out_sem) for i in range(4)]
     for i, j in blocks:
         pair = halves(folded(zeros[i, j]))
         far = times(jnp.concatenate(pair, axis=0), bs_buf[i, j])
@@ -334,15 +336,9 @@
         if j == 3:
             outs[i].start()
 
-    halo_do("s", left, False)
-    halo_do("0", left, False)
-    halo_do("1", left, False)
-    ring_do("2", left, False)
-    ring_do("3", left, False)
-    for d in range(3):
-        pair_copy(d).wait_send()
-    for copy in outs:
-        copy.wait()
+    for at in range(6):
+        left(at)
+    pltpu.make_async_copy(o_buf, out, out_sem).wait()
 
 
 def on_device(*args):
@@ -380,15 +376,21 @@
             vmem((16, 128), BF16),
             vmem((4, 16, 128), BF16),
             vmem((4, 4, 16, 256), F32),
+            vmem((4, 4, 16, 128), BF16),
+            vmem((4, 4, 16, 256), BF16),
+            vmem((6, 6, 16, 256), BF16),
+            vmem((8, 8, 16, 128), BF16),
+            vmem((6, 6, 16, 128), BF16),
+            vmem((5, 5, 16, 128), BF16),
+            vmem((5, 5, 16, 128), BF16),
             dma((9,)),
             dma((6,)),
-            dma((4,)),
+            dma,
             dma((5,)),
-            dma((4,)),
-        ]
-        + [dma((8,))] * 6
-        + [dma((16,))] * 4
-        + [dma((3,))] * 2,
+            dma,
+            dma((6,)),
+            dma((6,)),
+        ],
         compiler_params=pltpu.CompilerParams(
             collective_id=0, has_side_effects=True, vmem_limit_bytes=60 * 1024 * 1024
         ),

time: 22.2 us -> 21.1 us (0.950)
  Pallas kernels: 20.4 us -> 19.3 us
    pallas_call x1, Pallas kernels: 20.4 us -> 19.3 us  [on_device(): pl.pallas_call(kernel, out_shape=jax.ShapeDtypeStruct((4, 4, 16, 256), F3...]
where the time goes in v4:
time: 21.1 us; the launch traced here: 21 us
  Pallas kernels  19.3 us (91%)
  local copies, waits for them, and re-layouts  1.67 us (8%)
    pallas_call x1, Pallas kernels, on_device(): pl.pallas_call(kernel, out_shape=jax.ShapeDtypeStruct((4, 4, 16, 256), F3...  19.3 us
    unnamed x1, local copies, waits for them, and re-layouts  1.67 us

profile of v4, /device:TPU:1, one launch (start us, length us, event | category | flops | bytes accessed | tf_op | source)
XLA Modules:
  0.0 21.0 jit_solution(3275383077609942552)
XLA Ops:
  0.0 19.3 %patches.1 = f32[4,4,16,256]{3,2,1,0:T(8,128)} custom-call(bf16[4,4,16,256]{3,2,1,0:T(8,128)(2,1)} %sources.1, s32[4,4,5]{2,1,0:T(4,128)} %h_near.1, bf16[4,4,5,256,256]{4,3,2,1,0:T(8,128)(2,1)} %near_blocks.1, f32[4,4,64,256]{3,2,1,0:T(8,128)} %basis.1, f32[4,4,64,64]{3,2,1,0:T(8,128)} %one.1, f32[2,2,64,64]{3,2,1,0:T(8,128)} %two.1, ...), custom_call_target="tpu_custom_call" | custom-call | tf_op jit(solution)/shard_map/patches/pallas_call | solution.py:347
  19.3 1.7 %copy.17 = f32[4,4,16,256]{3,2,1,0:T(8,128)} copy(f32[4,4,16,256]{3,2,1,0:T(8,128)} %patches.1) | data formatting | bytes 524288

commit v5 on v4

--- a/solution.py
+++ b/solution.py
@@ -260,7 +260,6 @@
         load.start()
     loads[8].wait()
     arrived(0)
-    arrived(4)
 
     def near_edge(some):
         for i, j in some:
@@ -281,14 +280,16 @@
             total = term if total is None else total + term
         return total
 
-    loads[5].wait()
     for load in near_loads[2:4]:
         load.wait()
+    near_edge(edge[:4] + ((1, 0), (2, 0)))
+
+    loads[5].wait()
+    arrived(4)
     total = coupled(
         lambda k: c3_buf[k], lambda k: k_three[row3, col3, k], lambda u, v: p3[u, v]
     )
     part[0] = halves(folded(total))[0]
-    near_edge(edge[:4] + ((1, 0), (2, 0)))
     pair_send()
     for load in near_loads[4:]:
         load.wait()

time: 21.1 us -> 20.1 us (0.953)
  Pallas kernels: 19.3 us -> 18.3 us
    pallas_call x1, Pallas kernels: 19.3 us -> 18.3 us  [on_device(): pl.pallas_call(kernel, out_shape=jax.ShapeDtypeStruct((4, 4, 16, 256), F3...]
where the time goes in v5:
time: 20.1 us; the launch traced here: 19.9 us
  Pallas kernels  18.3 us (91%)
  local copies, waits for them, and re-layouts  1.67 us (8%)
    pallas_call x1, Pallas kernels, on_device(): pl.pallas_call(kernel, out_shape=jax.ShapeDtypeStruct((4, 4, 16, 256), F3...  18.3 us
    unnamed x1, local copies, waits for them, and re-layouts  1.67 us

profile of v5, /device:TPU:1, one launch (start us, length us, event | category | flops | bytes accessed | tf_op | source)
XLA Modules:
  0.0 19.9 jit_solution(10522409172100599944)
XLA Ops:
  0.0 18.3 %patches.1 = f32[4,4,16,256]{3,2,1,0:T(8,128)} custom-call(bf16[4,4,16,256]{3,2,1,0:T(8,128)(2,1)} %sources.1, s32[4,4,5]{2,1,0:T(4,128)} %h_near.1, bf16[4,4,5,256,256]{4,3,2,1,0:T(8,128)(2,1)} %near_blocks.1, f32[4,4,64,256]{3,2,1,0:T(8,128)} %basis.1, f32[4,4,64,64]{3,2,1,0:T(8,128)} %one.1, f32[2,2,64,64]{3,2,1,0:T(8,128)} %two.1, ...), custom_call_target="tpu_custom_call" | custom-call | tf_op jit(solution)/shard_map/patches/pallas_call | solution.py:348
  18.3 1.7 %copy.17 = f32[4,4,16,256]{3,2,1,0:T(8,128)} copy(f32[4,4,16,256]{3,2,1,0:T(8,128)} %patches.1) | data formatting | bytes 524288
